TPU v7x, 512 devices: a whole 4x8x8 slice. The times are simulated.
512 devices in a mesh: rep: 32 (over z, x), tp: 16 (over y, core).
Axes of the slice: x: 4, y: 8, z: 8, core: 2. Of those that a mesh axis runs over, the one named last changes fastest.
Arguments:
- hidden: bfloat16 [32768, 8192], P('rep', 'tp'), may hold values from -6 to 6
- grad_out: bfloat16 [32768, 2048], P('rep'), may hold values from -6 to 6
- weight: bfloat16 [32, 8192, 2048], P('rep', 'tp'), may hold values from -0.125 to 0.125
- alive: int32 [32, 16], replicated, may hold values from 0 to 1, as said below
Outputs:
- grad_hidden: bfloat16 [32768, 8192], P('rep', 'tp')
- grad_weight: float32 [7168, 2048], P('tp', 'rep')
Inputs may be any that keep to these rules, and one draw needn't show every extreme that they name: `alive`: exactly 8 replicas have exactly two zeros in their row; every other row is all ones.
All inputs are finite; a program needn't handle non-finite values.
Results may differ from a plain program's by a relative error of at most 0.001.
Values may be sent and summed in bfloat16 or wider, within the bound.
No kernel may reach another device: no remote copies, remote signals or barrier semaphores. Data moves between devices by JAX's collectives and lax.ppermute only.
A program may use at most 64 MiB of HBM per device.

v0:
```python
import jax
import jax.numpy as jnp
from jax import lax
from jax.sharding import PartitionSpec as P

FF = 7168


def from_behind(x, axis, by):
    size = lax.axis_size(axis)
    pairs = [(i, i + by) for i in range(size) if 0 <= i + by < size]
    return lax.ppermute(x, axis, pairs)


def local(hidden, grad_out, weight, alive):
    replica = lax.axis_index("rep")
    tensor_index = lax.axis_index("tp")
    tensor_count = lax.axis_size("tp")
    replica_count = lax.axis_size("rep")
    slot_width = hidden.shape[1]
    common_width = FF // tensor_count
    alive_row = lax.dynamic_slice_in_dim(alive, replica, 1, 0)[0]
    live_count = jnp.sum(alive_row)
    slice_width = FF // live_count
    live_rank = jnp.cumsum(alive_row) - alive_row
    self_alive = alive_row[tensor_index]
    product = lax.dot_general(
        grad_out, weight[0], (((1,), (1,)), ((), ())), preferred_element_type=jnp.float32
    )
    columns = jnp.arange(slot_width)
    usable = (columns < slice_width) & (self_alive == 1)
    grad_hidden = jnp.where(usable[None, :], product, 0.0).astype(jnp.bfloat16)

    def common_part(source_block, source_dev, receiver):
        present = (source_dev >= 0) & (source_dev < tensor_count)
        holder = jnp.clip(source_dev, 0, tensor_count - 1)
        offset_cols = common_width * receiver - live_rank[holder] * slice_width
        live_src = (alive_row[holder] == 1) & present
        padded = jnp.pad(source_block, ((0, 0), (slot_width, slot_width)))
        first_col = jnp.clip(offset_cols + slot_width, 0, 2 * slot_width)
        window = lax.dynamic_slice_in_dim(padded, first_col, common_width, 1)
        position = jnp.arange(common_width) + offset_cols
        wanted = (position >= 0) & (position < slice_width) & live_src
        return jnp.where(wanted[None, :], window, jnp.zeros((), jnp.bfloat16))

    common = common_part(hidden, tensor_index, tensor_index)
    for offset in (-2, -1, 1, 2):
        shifted = from_behind(hidden, "tp", -offset)
        common = common + common_part(shifted, tensor_index + offset, tensor_index)
    factor = float(replica_count * grad_out.shape[0]) ** (-0.5)
    partial_value = lax.dot_general(
        common, grad_out, (((0,), (0,)), ((), ())), preferred_element_type=jnp.float32
    )
    owned_sum = lax.psum_scatter(partial_value, "rep", scatter_dimension=1, tiled=True)
    return (grad_hidden, owned_sum * factor)


def solution(mesh):
    return jax.shard_map(
        local,
        mesh=mesh,
        in_specs=(P("rep", "tp"), P("rep", None), P("rep", "tp", None), P()),
        out_specs=(P("rep", "tp"), P("tp", "rep")),
        check_vma=False,
    )
```

profile of v0, /device:TPU:8, one launch (start us, length us, event | category | flops | bytes accessed | tf_op | source)
XLA Modules:
  0.0 302.6 jit_solution(14776529110736798936)
XLA Ops:
  7.2 0.0 copy-start
  7.2 0.0 reduce-scatter.2.cloned.1.call-start
  7.2 3.6 %collective-permute-start = (bf16[1024,512]{1,0:T(8,128)(2,1)}, bf16[1024,512]{1,0:T(8,128)(2,1)S(1)}, u32[]{:S(2)}, u32[]{:S(2)}) collective-permute-start(bf16[1024,512]{1,0:T(8,128)(2,1)} %param.4), channel_id=1, source_target_pairs={{0,2},{1,3},{2,4},{3,5},{4,6},{5,7},{6,8},{7,9},{8,10},{9,11},{10,... | collective-permute-start | bytes 3145736 | tf_op jit(solution)/shard_map/ppermute | solution.py:12
  10.8 1.9 collective-permute-start.1
  12.8 3.6 %collective-permute-start.2 = (bf16[1024,512]{1,0:T(8,128)(2,1)}, bf16[1024,512]{1,0:T(8,128)(2,1)}, u32[]{:S(2)}, u32[]{:S(2)}) collective-permute-start(bf16[1024,512]{1,0:T(8,128)(2,1)} %param.4), channel_id=1, source_target_pairs={{1,0},{2,1},{3,2},{4,3},{5,4},{6,5},{7,6},{8,7},{9,8},{10,9},{11,1... | collective-permute-start | bytes 3145736 | tf_op jit(solution)/shard_map/ppermute | solution.py:12
  16.4 3.6 %collective-permute-start.3 = (bf16[1024,512]{1,0:T(8,128)(2,1)}, bf16[1024,512]{1,0:T(8,128)(2,1)}, u32[]{:S(2)}, u32[]{:S(2)}) collective-permute-start(bf16[1024,512]{1,0:T(8,128)(2,1)} %param.4), channel_id=1, source_target_pairs={{2,0},{3,1},{4,2},{5,3},{6,4},{7,5},{8,6},{9,7},{10,8},{11,9},{12,... | collective-permute-start | bytes 3145736 | tf_op jit(solution)/shard_map/ppermute | solution.py:12
  20.0 1.4 dynamic-slice_reduce_fusion
  23.5 0.1 reduce.1
  23.6 0.7 fusion.49
  25.6 1.6 fusion.48
  32.4 6.4 %collective-permute-done = bf16[1024,512]{1,0:T(8,128)(2,1)S(1)} collective-permute-done((bf16[1024,512]{1,0:T(8,128)(2,1)}, bf16[1024,512]{1,0:T(8,128)(2,1)S(1)}, u32[]{:S(2)}, u32[]{:S(2)}) %collective-permute-start) | collective-permute-done | bytes 1048608 | tf_op jit(solution)/shard_map/ppermute | solution.py:12
  38.7 7.0 %collective-permute-done.1 = bf16[1024,512]{1,0:T(8,128)(2,1)} collective-permute-done((bf16[1024,512]{1,0:T(8,128)(2,1)}, bf16[1024,512]{1,0:T(8,128)(2,1)}, u32[]{:S(2)}, u32[]{:S(2)}) %collective-permute-start.1) | collective-permute-done | bytes 1048608 | tf_op jit(solution)/shard_map/ppermute | solution.py:12
  45.7 0.0 collective-permute-done.2
  45.7 7.8 %collective-permute-done.3 = bf16[1024,512]{1,0:T(8,128)(2,1)} collective-permute-done((bf16[1024,512]{1,0:T(8,128)(2,1)}, bf16[1024,512]{1,0:T(8,128)(2,1)}, u32[]{:S(2)}, u32[]{:S(2)}) %collective-permute-start.3) | collective-permute-done | bytes 1048608 | tf_op jit(solution)/shard_map/ppermute | solution.py:12
  53.5 9.4 %fusion.9 = f32[448,2048]{0,1:T(8,128)} fusion(bf16[1024,2048]{1,0:T(8,128)(2,1)} %param.5, s32[]{:T(128)S(6)} %min.43, bf16[1024,512]{1,0:T(8,128)(2,1)} %param.4, s32[]{:T(128)S(6)} %min.46, bf16[1024,512]{1,0:T(8,128)(2,1)S(1)} %collective-permute-done, s32[]{:T(128)S(6)} %min.49, bf16[1024,512]{1,0:T(8,128)(2,1)} %collective-permute-done.1, ...), kind=kOutput, calls=%fused_computation.13 | convolution fusion | flops 1885929472 | bytes 13109460 | tf_op jit(solution)/shard_map/dot_general | solution.py:51
  63.0 0.0 reduce-scatter.2.cloned.1.call-update
  63.7 0.0 copy-done
  63.7 5.5 %select_convert_fusion = bf16[1024,512]{1,0:T(8,128)(2,1)} fusion(bf16[1024,2048]{1,0:T(8,128)(2,1)} %param.5, bf16[1,512,2048]{2,1,0:T(8,128)(2,1)S(1)} %copy-done, pred[512]{0:T(512)(128)(4,1)S(1)} %fusion.45), kind=kOutput, calls=%fused_computation.7 | convolution fusion | flops 2148532224 | bytes 7340544 | tf_op jit(solution)/shard_map/dot_general | solution.py:27
  69.2 224.9 %reduce-scatter.2.cloned.1.call-done = f32[448,64]{0,1:T(8,128)} async-done(((f32[448,2048]{0,1:T(8,128)}), f32[448,64]{0,1:T(8,128)}) %reduce-scatter.2.cloned.1.call-update) | async-done | bytes 114704 | tf_op jit(solution)/shard_map/reduce_scatter | solution.py:54
  294.2 1.6 broadcast_multiply_fusion
  (6 shorter events, 0.1 us)
Async XLA Ops:
  7.2 56.5 %copy-start = (bf16[1,512,2048]{2,1,0:T(8,128)(2,1)S(1)}, bf16[1,512,2048]{2,1,0:T(8,128)(2,1)}, u32[]{:S(2)}) copy-start(bf16[1,512,2048]{2,1,0:T(8,128)(2,1)} %param.6) | copy-start | bytes 6291460
  7.2 287.0 %reduce-scatter.2.cloned.1.call-start = ((), (), s32[]{:S(2)}) async-start(), calls=%async_computation.1 | async-start | bytes 4325376 | tf_op jit(solution)/shard_map/reduce_scatter | solution.py:54
  7.2 31.5 %collective-permute-start = (bf16[1024,512]{1,0:T(8,128)(2,1)}, bf16[1024,512]{1,0:T(8,128)(2,1)S(1)}, u32[]{:S(2)}, u32[]{:S(2)}) collective-permute-start(bf16[1024,512]{1,0:T(8,128)(2,1)} %param.4), channel_id=1, source_target_pairs={{0,2},{1,3},{2,4},{3,5},{4,6},{5,7},{6,8},{7,9},{8,10},{9,11},{10,... | collective-permute-start | bytes 3145736 | tf_op jit(solution)/shard_map/ppermute | solution.py:12
  10.8 34.9 %collective-permute-start.1 = (bf16[1024,512]{1,0:T(8,128)(2,1)}, bf16[1024,512]{1,0:T(8,128)(2,1)}, u32[]{:S(2)}, u32[]{:S(2)}) collective-permute-start(bf16[1024,512]{1,0:T(8,128)(2,1)} %param.4), channel_id=1, source_target_pairs={{0,1},{1,2},{2,3},{3,4},{4,5},{5,6},{6,7},{7,8},{8,9},{9,10},{10,1... | collective-permute-start | bytes 3145736 | tf_op jit(solution)/shard_map/ppermute | solution.py:12
  12.8 32.9 %collective-permute-start.2 = (bf16[1024,512]{1,0:T(8,128)(2,1)}, bf16[1024,512]{1,0:T(8,128)(2,1)}, u32[]{:S(2)}, u32[]{:S(2)}) collective-permute-start(bf16[1024,512]{1,0:T(8,128)(2,1)} %param.4), channel_id=1, source_target_pairs={{1,0},{2,1},{3,2},{4,3},{5,4},{6,5},{7,6},{8,7},{9,8},{10,9},{11,1... | collective-permute-start | bytes 3145736 | tf_op jit(solution)/shard_map/ppermute | solution.py:12
  16.4 37.1 %collective-permute-start.3 = (bf16[1024,512]{1,0:T(8,128)(2,1)}, bf16[1024,512]{1,0:T(8,128)(2,1)}, u32[]{:S(2)}, u32[]{:S(2)}) collective-permute-start(bf16[1024,512]{1,0:T(8,128)(2,1)} %param.4), channel_id=1, source_target_pairs={{2,0},{3,1},{4,2},{5,3},{6,4},{7,5},{8,6},{9,7},{10,8},{11,9},{12,... | collective-permute-start | bytes 3145736 | tf_op jit(solution)/shard_map/ppermute | solution.py:12
Sparse Core Ops, SparseCore 0:
  63.1 231.0 reduce-scatter.1
where the time goes:
time: 303 us
  waiting for transfers between devices  246 us (81%)
  between operations  23.2 us (8%)
  matrix products  14.9 us (5%)
  starting transfers between devices  12.8 us (4%)
  other arithmetic  3.18 us (1%)
    reduce_scatter x1, waiting for transfers between devices, local(): lax.psum_scatter(partial_value, 'rep', scatter_dimension=1, tiled=True)  225 us
    ppermute x4, waiting for transfers between devices, from_behind(): return lax.ppermute(x, axis, pairs)  21.2 us
    ppermute x4, starting transfers between devices, from_behind(): return lax.ppermute(x, axis, pairs)  12.8 us
    dot_general x1, matrix products, local(): lax.dot_general(common, grad_out, (((0,), (0,)), ((), ())), preferred_ele...  9.42 us
  transfers between devices with their start and end apart: 5, of which 4 were waited for; matrix products, arithmetic and copies ran while one was open for 3% of the time, Pallas kernels for 0%

commit v1 on v0

v1 whole, which is shorter than its diff:
```python
import functools

import jax
import jax.numpy as jnp
from jax import lax
from jax.experimental import pallas as pl
from jax.experimental.pallas import tpu as pltpu
from jax.sharding import PartitionSpec as P

FF = 7168
TOK, D, SLOT, COMMON = 1024, 2048, 512, 448
N_REP, N_TP = 32, 16
NEAR, FAR = 8, 4
ROWS = 224
GROUPS = ((0, 64), (64, 64), (128, 64), (192, 32))
PAD = 16
LOG_LEVELS = 14.999
FACTOR = float(N_REP * TOK) ** -0.5
F32, BF16, I16 = jnp.float32, jnp.bfloat16, jnp.int16
VMEM = pl.BlockSpec(memory_space=pltpu.VMEM)
SMEM = pl.BlockSpec(memory_space=pltpu.SMEM)


def layout(where, alive):
    replica = where[0]
    live = jnp.int32(0)
    for t in range(N_TP):
        live += alive[replica, t]
    width = lax.div(jnp.int32(FF), live)

    def holds(device):
        rank = jnp.int32(0)
        for t in range(N_TP):
            rank += jnp.where(t < device, alive[replica, t], 0)
        return alive[replica, device], rank * width

    return width, holds


def selection(width, held, first_wanted):
    is_alive, first_held = held
    rows = lax.broadcasted_iota(jnp.int32, (SLOT, COMMON), 0)
    cols = lax.broadcasted_iota(jnp.int32, (SLOT, COMMON), 1)
    shift = jnp.where(is_alive == 1, first_wanted - first_held, 4 * FF)
    return ((rows - cols == shift) & (rows < width)).astype(F32).astype(BF16)


def pick(own, other, sel_own, sel_other):
    got = jnp.dot(own, sel_own, preferred_element_type=F32)
    got += jnp.dot(other, sel_other, preferred_element_type=F32)
    return got.astype(BF16)


def windows_kernel(where, alive, own, other, right, left):
    width, holds = layout(where, alive)
    me = where[1]
    mine, theirs = holds(me), holds(me ^ 1)
    for out, to in ((right, me + 2), (left, me - 2)):
        first = to * COMMON
        sels = selection(width, mine, first), selection(width, theirs, first)
        for i in range(0, TOK, 256):
            out[i : i + 256] = pick(own[i : i + 256], other[i : i + 256], *sels)


def hidden_kernel(where, alive, grad, weight, own, other, grad_hidden, grad_t, local):
    width, holds = layout(where, alive)
    me = where[1]
    mine, theirs = holds(me), holds(me ^ 1)
    block = grad[...]
    product = lax.dot_general(block, weight[...], (((1,), (1,)), ((), ())), preferred_element_type=F32)
    cols = lax.broadcasted_iota(jnp.int32, product.shape, 1)
    limit = jnp.where(mine[0] == 1, width, 0)
    grad_hidden[...] = jnp.where(cols < limit, product, 0.0).astype(BF16)
    first = me * COMMON
    local[...] = pick(
        own[...], other[...], selection(width, mine, first), selection(width, theirs, first)
    )
    grad_t[...] = block.T


def steps_of(most):
    return jnp.ceil(256.0 * (jnp.log2(jnp.maximum(most, 1e-30)) - LOG_LEVELS))


def coded(value, inverse):
    return jnp.round(value * inverse).astype(jnp.int32).astype(I16)


def fold(product):
    groups = [product[:, c * 128 : c * 128 + 128] for c in range(3)]
    last = product[:, 384:]
    return groups + [last[:32] + pltpu.roll(last[32:], 64, 1)]


def tallest(value):
    return jnp.max(jnp.abs(value).reshape(value.shape[0] // 8, 8, 128), axis=0)


def write_code(out, index, blocks, folded, most):
    steps = [steps_of(jnp.max(m, axis=0, keepdims=True)) for m in most]
    inverse = [jnp.exp2(step * (-1.0 / 256.0)) for step in steps]
    for block in range(blocks):
        for (row, rows), inv in zip(GROUPS, inverse):
            r = block * ROWS + row
            out[index, r : r + rows] = coded(folded(r, rows), inv)
    head = jnp.concatenate(steps + [jnp.zeros((PAD - len(steps), 128), F32)], axis=0)
    out[index, blocks * ROWS :] = head.astype(jnp.int32).astype(I16)


def read_steps(got, index, blocks):
    head = got[index, blocks * ROWS :].astype(jnp.int32).astype(F32)
    return jnp.exp2(head * (1.0 / 256.0))


def read_sum(got, sources, steps, r, rows, group):
    value = None
    for k in range(sources):
        term = got[k, r : r + rows].astype(jnp.int32).astype(F32) * steps[k][group : group + 1]
        value = term if value is None else value + term
    return value


def partial_kernel(grad_t, local, from_left, from_right, out, common, folded):
    common[:, :COMMON] = local[...] + from_left[...] + from_right[...]
    common[:, COMMON:] = jnp.zeros((TOK, SLOT - COMMON), BF16)
    step = 256
    most = [[None] * len(GROUPS) for _ in range(NEAR)]
    for f in range(0, D, step):
        got = jnp.dot(grad_t[f : f + step], common[...], preferred_element_type=F32)
        for owner in range(f // 64, (f + step) // 64):
            far, near = owner // NEAR, owner % NEAR
            parts = fold(got[owner * 64 - f : owner * 64 - f + 64])
            for g, ((row, rows), part) in enumerate(zip(GROUPS, parts)):
                folded[near, far * ROWS + row : far * ROWS + row + rows] = part
                big = tallest(part)
                most[near][g] = big if far == 0 else jnp.maximum(most[near][g], big)
    for near in range(NEAR):
        write_code(out, near, FAR, lambda r, rows: folded[near, r : r + rows], most[near])


def middle_kernel(got, out, folded):
    steps = [read_steps(got, k, FAR) for k in range(NEAR)]
    for far in range(FAR):
        most = []
        for g, (row, rows) in enumerate(GROUPS):
            value = read_sum(got, NEAR, steps, far * ROWS + row, rows, g)
            folded[row : row + rows] = value
            most.append(tallest(value))
        write_code(out, far, 1, lambda r, rows: folded[r : r + rows], most)


def final_kernel(got, out):
    steps = [read_steps(got, k, 1) * FACTOR for k in range(FAR)]
    parts = [read_sum(got, FAR, steps, row, rows, g) for g, (row, rows) in enumerate(GROUPS)]
    for c in range(3):
        out[:, c * 128 : c * 128 + 128] = parts[c]
    out[:32, 384:] = parts[3][:, :64]
    out[32:, 384:] = pltpu.roll(parts[3], 64, 1)[:, :64]


def shape(dims, kind):
    return jax.ShapeDtypeStruct(dims, kind)


def params(mib):
    return pltpu.CompilerParams(vmem_limit_bytes=mib << 20)


def local(hidden, grad_out, weight, alive):
    where = jnp.stack([lax.axis_index("rep"), lax.axis_index("tp")]).astype(jnp.int32)
    other = lax.ppermute(hidden, "tp", [(t, t ^ 1) for t in range(N_TP)])
    right, left = pl.pallas_call(
        windows_kernel,
        out_shape=[shape((TOK, COMMON), BF16)] * 2,
        in_specs=[SMEM, SMEM, VMEM, VMEM],
        out_specs=[VMEM, VMEM],
        compiler_params=params(24),
        name="windows",
    )(where, alive, hidden, other)
    from_left = lax.ppermute(right, "tp", [(t, t + 2) for t in range(14) if t % 2 == 0 or t >= 6])
    from_right = lax.ppermute(left, "tp", [(t, t - 2) for t in range(2, 16) if t % 2 == 1 or t <= 8])
    step = 256
    grad_hidden, grad_t, own = pl.pallas_call(
        hidden_kernel,
        grid=(TOK // step,),
        out_shape=[shape((TOK, SLOT), BF16), shape((D, TOK), BF16), shape((TOK, COMMON), BF16)],
        in_specs=[
            SMEM,
            SMEM,
            pl.BlockSpec((step, D), lambda i: (i, 0)),
            pl.BlockSpec((SLOT, D), lambda i: (0, 0)),
            pl.BlockSpec((step, SLOT), lambda i: (i, 0)),
            pl.BlockSpec((step, SLOT), lambda i: (i, 0)),
        ],
        out_specs=[
            pl.BlockSpec((step, SLOT), lambda i: (i, 0)),
            pl.BlockSpec((D, step), lambda i: (0, i)),
            pl.BlockSpec((step, COMMON), lambda i: (i, 0)),
        ],
        compiler_params=params(24),
        cost_estimate=pl.CostEstimate(flops=2 * TOK * SLOT * (D + 2 * COMMON), bytes_accessed=16 << 20, transcendentals=0),
        name="hidden_grad",
    )(where, alive, grad_out, weight[0], hidden, other)
    payload = pl.pallas_call(
        partial_kernel,
        out_shape=shape((NEAR, FAR * ROWS + PAD, 128), I16),
        in_specs=[VMEM] * 4,
        out_specs=VMEM,
        scratch_shapes=[pltpu.VMEM((TOK, SLOT), BF16), pltpu.VMEM((NEAR, FAR * ROWS, 128), F32)],
        compiler_params=params(32),
        name="partial",
    )(grad_t, own, from_left, from_right)
    payload = lax.all_to_all(
        payload, "rep", 0, 0, axis_index_groups=[[f * NEAR + n for n in range(NEAR)] for f in range(FAR)]
    )
    payload = pl.pallas_call(
        middle_kernel,
        out_shape=shape((FAR, ROWS + PAD, 128), I16),
        in_specs=[VMEM],
        out_specs=VMEM,
        scratch_shapes=[pltpu.VMEM((ROWS, 128), F32)],
        compiler_params=params(16),
        name="middle",
    )(payload)
    payload = lax.all_to_all(
        payload, "rep", 0, 0, axis_index_groups=[[f * NEAR + n for f in range(FAR)] for n in range(NEAR)]
    )
    grad_weight_t = pl.pallas_call(
        final_kernel,
        out_shape=shape((64, COMMON), F32),
        in_specs=[VMEM],
        out_specs=VMEM,
        compiler_params=params(16),
        name="final",
    )(payload)
    return grad_hidden, grad_weight_t.T


def solution(mesh):
    return jax.shard_map(
        local,
        mesh=mesh,
        in_specs=(P("rep", "tp"), P("rep", None), P("rep", "tp", None), P()),
        out_specs=(P("rep", "tp"), P("tp", "rep")),
        check_vma=False,
    )
```

time: 303 us -> 104 us (0.34)
  the two profiles are of different devices: /device:TPU:8 before, /device:TPU:24 now
where the time goes in v1:
time: 104 us; the launch traced here: 103 us
  blocking collectives  49.6 us (48%)
  local copies, waits for them, and re-layouts  17.5 us (17%)
  Pallas kernels  13.5 us (13%)
  waiting for transfers between devices  13.3 us (13%)
  starting transfers between devices  8.52 us (8%)
    all_to_all x2, blocking collectives, local(): lax.all_to_all(payload, 'rep', 0, 0, axis_index_groups=[[f * NEAR + n for...  49.6 us
    unnamed x15, local copies, waits for them, and re-layouts  10.9 us
    ppermute x1, waiting for transfers between devices, local(): lax.ppermute(left, 'tp', [(t, t - 2) for t in range(2, 16) if t % 2 == 1...  6.1 us
    pallas_call x1, Pallas kernels, local(): pl.pallas_call(hidden_kernel, grid=(TOK // step,), out_shape=[shape((TOK,...  6.04 us
    ppermute x1, waiting for transfers between devices, local(): lax.ppermute(right, 'tp', [(t, t + 2) for t in range(14) if t % 2 == 0 or...  5.2 us
    ppermute x1, starting transfers between devices, local(): lax.ppermute(right, 'tp', [(t, t + 2) for t in range(14) if t % 2 == 0 or...  4.68 us
    pallas_call x2, local copies, waits for them, and re-layouts, local(): pl.pallas_call(windows_kernel, out_shape=[shape((TOK, COMMON), BF16)] * 2...  3.66 us
    pallas_call x1, Pallas kernels, local(): pl.pallas_call(windows_kernel, out_shape=[shape((TOK, COMMON), BF16)] * 2...  3.27 us
  transfers between devices with their start and end apart: 3, of which 3 were waited for; matrix products, arithmetic and copies ran while one was open for 3% of the time, Pallas kernels for 6%

profile of v1, /device:TPU:24, one launch (start us, length us, event | category | flops | bytes accessed | tf_op | source)
XLA Modules:
  0.0 103.1 jit_solution(2208485074596260109)
XLA Ops:
  0.6 1.9 %collective-permute-start = (bf16[1024,512]{1,0:T(8,128)(2,1)}, bf16[1024,512]{1,0:T(8,128)(2,1)S(1)}, u32[]{:S(2)}, u32[]{:S(2)}) collective-permute-start(bf16[1024,512]{1,0:T(8,128)(2,1)} %own.3), channel_id=1, source_target_pairs={{0,1},{1,0},{2,3},{3,2},{4,5},{5,4},{6,7},{7,6},{8,9},{9,8},{10,11... | collective-permute-start | bytes 3145736 | tf_op jit(solution)/shard_map/ppermute | solution.py:171
  2.6 0.8 copy.8.alive
  3.3 0.1 pad_add_fusion.where
  3.4 2.0 %collective-permute-done.other = bf16[1024,512]{1,0:T(8,128)(2,1)S(1)} collective-permute-done((bf16[1024,512]{1,0:T(8,128)(2,1)}, bf16[1024,512]{1,0:T(8,128)(2,1)S(1)}, u32[]{:S(2)}, u32[]{:S(2)}) %collective-permute-start) | collective-permute-done | bytes 1048608 | tf_op jit(solution)/shard_map/ppermute | solution.py:171
  5.4 0.0 copy-start.2
  5.4 1.2 %copy-done.2 = bf16[1024,512]{1,0:T(8,128)(2,1)S(1)} copy-done((bf16[1024,512]{1,0:T(8,128)(2,1)S(1)}, bf16[1024,512]{1,0:T(8,128)(2,1)}, u32[]{:S(2)}) %copy-start.2) | copy-done | bytes 1048600
  6.6 3.3 %windows.1 = (bf16[1024,448]{1,0:T(8,128)(2,1)S(1)}, bf16[1024,448]{1,0:T(8,128)(2,1)S(1)}) custom-call(s32[2]{0:T(128)S(1)} %pad_add_fusion.where, s32[32,16]{1,0:T(8,128)S(1)} %copy.8.alive, bf16[1024,512]{1,0:T(8,128)(2,1)S(1)} %copy-done.2, bf16[1024,512]{1,0:T(8,128)(2,1)S(1)} %collective-permute-done.other), custom_call_target="tpu_custom_call" | custom-call | tf_op jit(solution)/shard_map/windows/pallas_call | solution.py:172
  9.9 0.0 copy-start.4
  9.9 1.0 copy-done.4
  10.9 0.0 copy-start.3
  10.9 2.4 %copy.10 = bf16[1024,448]{0,1:T(8,128)(2,1)} copy(bf16[1024,448]{1,0:T(8,128)(2,1)} %copy-done.4) | data formatting | bytes 1835008 | tf_op jit(solution)/shard_map/windows/pallas_call | solution.py:172
  13.2 4.7 %collective-permute-start.1 = (bf16[1024,448]{0,1:T(8,128)(2,1)}, bf16[1024,448]{0,1:T(8,128)(2,1)}, u32[]{:S(2)}, u32[]{:S(2)}) collective-permute-start(bf16[1024,448]{0,1:T(8,128)(2,1)} %copy.10), channel_id=1, source_target_pairs={{0,2},{2,4},{4,6},{6,8},{7,9},{8,10},{9,11},{10,12},{11,13},{12,14... | collective-permute-start | bytes 2752520 | tf_op jit(solution)/shard_map/ppermute | solution.py:180
  17.9 1.3 %copy.11 = bf16[1024,448]{0,1:T(8,128)(2,1)} copy(bf16[1024,448]{1,0:T(8,128)(2,1)S(1)} %get-tuple-element.11) | data formatting | bytes 1835008 | tf_op jit(solution)/shard_map/windows/pallas_call | solution.py:172
  19.2 1.9 %collective-permute-start.2 = (bf16[1024,448]{0,1:T(8,128)(2,1)}, bf16[1024,448]{0,1:T(8,128)(2,1)}, u32[]{:S(2)}, u32[]{:S(2)}) collective-permute-start(bf16[1024,448]{0,1:T(8,128)(2,1)} %copy.11), channel_id=1, source_target_pairs={{2,0},{3,1},{4,2},{5,3},{6,4},{7,5},{8,6},{9,7},{11,9},{13,11},{15... | collective-permute-start | bytes 2752520 | tf_op jit(solution)/shard_map/ppermute | solution.py:181
  21.1 0.0 copy-done.3
  21.1 0.0 copy-start.5
  21.2 2.2 %copy-done.5 = bf16[1024,2048]{1,0:T(8,128)(2,1)S(1)} copy-done((bf16[1024,2048]{1,0:T(8,128)(2,1)S(1)}, bf16[1024,2048]{1,0:T(8,128)(2,1)}, u32[]{:S(2)}) %copy-start.5) | copy-done | bytes 4194328
  23.3 0.0 copy-start.6
  23.3 1.6 %copy-done.6 = bf16[1,512,2048]{2,1,0:T(8,128)(2,1)S(1)} copy-done((bf16[1,512,2048]{2,1,0:T(8,128)(2,1)S(1)}, bf16[1,512,2048]{2,1,0:T(8,128)(2,1)}, u32[]{:S(2)}) %copy-start.6) | copy-done | bytes 2097176
  24.9 6.0 %hidden_grad.1 = (bf16[1024,512]{1,0:T(8,128)(2,1)}, bf16[2048,1024]{1,0:T(8,128)(2,1)S(1)}, bf16[1024,448]{1,0:T(8,128)(2,1)S(1)}) custom-call(s32[2]{0:T(128)S(1)} %pad_add_fusion.where, s32[32,16]{1,0:T(8,128)S(1)} %copy.8.alive, bf16[1024,2048]{1,0:T(8,128)(2,1)S(1)} %copy-done.5, bf16[512,2048]{1,0:T(8,128)(2,1)S(1)} %bitcast.4, ...), custom_call_target="tpu_custom_call" | custom-call | flops 3087007744 | bytes 16777216 | tf_op jit(solution)/shard_map/hidden_grad/pallas_call | solution.py:183
  31.0 2.0 %copy-done = bf16[2048,1024]{1,0:T(8,128)(2,1)} copy-done((bf16[2048,1024]{1,0:T(8,128)(2,1)}, bf16[2048,1024]{1,0:T(8,128)(2,1)S(1)}, u32[]{:S(2)}) %copy-start) | copy-done | bytes 4194328
  32.9 5.2 %collective-permute-done.1 = bf16[1024,448]{0,1:T(8,128)(2,1)} collective-permute-done((bf16[1024,448]{0,1:T(8,128)(2,1)}, bf16[1024,448]{0,1:T(8,128)(2,1)}, u32[]{:S(2)}, u32[]{:S(2)}) %collective-permute-start.1) | collective-permute-done | bytes 917536 | tf_op jit(solution)/shard_map/ppermute | solution.py:180
  38.1 1.5 %copy.12.from_left = bf16[1024,448]{1,0:T(8,128)(2,1)S(1)} copy(bf16[1024,448]{0,1:T(8,128)(2,1)} %collective-permute-done.1) | data formatting | bytes 1835008 | tf_op jit(solution)/shard_map/ppermute | solution.py:180
  39.6 6.1 %collective-permute-done.2 = bf16[1024,448]{0,1:T(8,128)(2,1)} collective-permute-done((bf16[1024,448]{0,1:T(8,128)(2,1)}, bf16[1024,448]{0,1:T(8,128)(2,1)}, u32[]{:S(2)}, u32[]{:S(2)}) %collective-permute-start.2) | collective-permute-done | bytes 917536 | tf_op jit(solution)/shard_map/ppermute | solution.py:181
  45.7 1.5 %copy.13.from_right = bf16[1024,448]{1,0:T(8,128)(2,1)S(1)} copy(bf16[1024,448]{0,1:T(8,128)(2,1)} %collective-permute-done.2) | data formatting | bytes 1835008 | tf_op jit(solution)/shard_map/ppermute | solution.py:181
  47.2 0.0 copy-start.1
  47.2 2.2 %copy-done.1 = bf16[2048,1024]{1,0:T(8,128)(2,1)S(1)} copy-done((bf16[2048,1024]{1,0:T(8,128)(2,1)S(1)}, bf16[2048,1024]{1,0:T(8,128)(2,1)}, u32[]{:S(2)}) %copy-start.1) | copy-done | bytes 4194328
  49.3 2.8 %partial.1 = s16[8,912,128]{2,1,0:T(8,128)(2,1)S(1)} custom-call(bf16[2048,1024]{1,0:T(8,128)(2,1)S(1)} %copy-done.1, bf16[1024,448]{1,0:T(8,128)(2,1)S(1)} %get-tuple-element.9.local, bf16[1024,448]{1,0:T(8,128)(2,1)S(1)} %copy.12.from_left, bf16[1024,448]{1,0:T(8,128)(2,1)S(1)} %copy.13.from_right), custom_call_target="tpu_custom_call" | custom-call | tf_op jit(solution)/shard_map/partial/pallas_call | solution.py:204
  52.2 31.0 %all_to_all.10.got = s16[8,912,128]{2,1,0:T(8,128)(2,1)S(1)} all-to-all(s16[8,912,128]{2,1,0:T(8,128)(2,1)S(1)} %partial.1), channel_id=1, replica_groups={{0,16,32,48,64,80,96,112},{128,144,160,176,192,208,224,240},{256,272,28..., dimensions={0} | all-to-all | bytes 3735552 | tf_op jit(solution)/shard_map/all_to_all | solution.py:213
  83.2 0.6 middle.1
  83.7 18.6 %all_to_all.11.got = s16[4,240,128]{2,1,0:T(8,128)(2,1)S(1)} all-to-all(s16[4,240,128]{2,1,0:T(8,128)(2,1)S(1)} %middle.1), channel_id=1, replica_groups={{0,128,256,384},{16,144,272,400},{32,160,288,416},{48,176,304,432},{64,..., dimensions={0} | all-to-all | bytes 491520 | tf_op jit(solution)/shard_map/all_to_all | solution.py:225
  102.3 0.8 final.1
  (1 shorter events, 0.0 us)
Async XLA Ops:
  0.6 4.8 %collective-permute-start = (bf16[1024,512]{1,0:T(8,128)(2,1)}, bf16[1024,512]{1,0:T(8,128)(2,1)S(1)}, u32[]{:S(2)}, u32[]{:S(2)}) collective-permute-start(bf16[1024,512]{1,0:T(8,128)(2,1)} %own.3), channel_id=1, source_target_pairs={{0,1},{1,0},{2,3},{3,2},{4,5},{5,4},{6,7},{7,6},{8,9},{9,8},{10,11... | collective-permute-start | bytes 3145736 | tf_op jit(solution)/shard_map/ppermute | solution.py:171
  5.4 1.2 %copy-start.2 = (bf16[1024,512]{1,0:T(8,128)(2,1)S(1)}, bf16[1024,512]{1,0:T(8,128)(2,1)}, u32[]{:S(2)}) copy-start(bf16[1024,512]{1,0:T(8,128)(2,1)} %own.3) | copy-start | bytes 3145732
  9.9 1.0 copy-start.4
  10.9 10.3 %copy-start.3 = (bf16[1024,512]{1,0:T(8,128)(2,1)S(1)}, bf16[1024,512]{1,0:T(8,128)(2,1)}, u32[]{:S(2)}) copy-start(bf16[1024,512]{1,0:T(8,128)(2,1)} %own.3) | copy-start | bytes 3145732
  13.2 24.9 %collective-permute-start.1 = (bf16[1024,448]{0,1:T(8,128)(2,1)}, bf16[1024,448]{0,1:T(8,128)(2,1)}, u32[]{:S(2)}, u32[]{:S(2)}) collective-permute-start(bf16[1024,448]{0,1:T(8,128)(2,1)} %copy.10), channel_id=1, source_target_pairs={{0,2},{2,4},{4,6},{6,8},{7,9},{8,10},{9,11},{10,12},{11,13},{12,14... | collective-permute-start | bytes 2752520 | tf_op jit(solution)/shard_map/ppermute | solution.py:180
  19.2 26.5 %collective-permute-start.2 = (bf16[1024,448]{0,1:T(8,128)(2,1)}, bf16[1024,448]{0,1:T(8,128)(2,1)}, u32[]{:S(2)}, u32[]{:S(2)}) collective-permute-start(bf16[1024,448]{0,1:T(8,128)(2,1)} %copy.11), channel_id=1, source_target_pairs={{2,0},{3,1},{4,2},{5,3},{6,4},{7,5},{8,6},{9,7},{11,9},{13,11},{15... | collective-permute-start | bytes 2752520 | tf_op jit(solution)/shard_map/ppermute | solution.py:181
  21.1 2.2 %copy-start.5 = (bf16[1024,2048]{1,0:T(8,128)(2,1)S(1)}, bf16[1024,2048]{1,0:T(8,128)(2,1)}, u32[]{:S(2)}) copy-start(bf16[1024,2048]{1,0:T(8,128)(2,1)} %grad.1) | copy-start | bytes 12582916
  23.3 1.6 %copy-start.6 = (bf16[1,512,2048]{2,1,0:T(8,128)(2,1)S(1)}, bf16[1,512,2048]{2,1,0:T(8,128)(2,1)}, u32[]{:S(2)}) copy-start(bf16[1,512,2048]{2,1,0:T(8,128)(2,1)} %param.6) | copy-start | bytes 6291460
  31.0 2.0 %copy-start = (bf16[2048,1024]{1,0:T(8,128)(2,1)}, bf16[2048,1024]{1,0:T(8,128)(2,1)S(1)}, u32[]{:S(2)}) copy-start(bf16[2048,1024]{1,0:T(8,128)(2,1)S(1)} %get-tuple-element.8.grad_t) | copy-start | bytes 12582916
  47.2 2.2 %copy-start.1 = (bf16[2048,1024]{1,0:T(8,128)(2,1)S(1)}, bf16[2048,1024]{1,0:T(8,128)(2,1)}, u32[]{:S(2)}) copy-start(bf16[2048,1024]{1,0:T(8,128)(2,1)} %copy-done) | copy-start | bytes 12582916

commit v2 on v1

v2 whole, which is shorter than its diff:
```python
import functools

import jax
import jax.numpy as jnp
from jax import lax
from jax.experimental import pallas as pl
from jax.experimental.pallas import tpu as pltpu
from jax.sharding import PartitionSpec as P

FF = 7168
TOK, D, SLOT, COMMON = 1024, 2048, 512, 448
N_REP, N_TP = 32, 16
NEAR, FAR = 8, 4
ROWS = 224
GROUPS = ((0, 64), (64, 64), (128, 64), (192, 32))
PAD = 16
LOG_LEVELS = 14.999
FACTOR = float(N_REP * TOK) ** -0.5
F32, BF16, I16 = jnp.float32, jnp.bfloat16, jnp.int16
VMEM = pl.BlockSpec(memory_space=pltpu.VMEM)
SMEM = pl.BlockSpec(memory_space=pltpu.SMEM)


def layout(where, alive):
    replica = where[0]
    live = jnp.int32(0)
    for t in range(N_TP):
        live += alive[t, replica]
    width = lax.div(jnp.int32(FF), live)

    def holds(device):
        rank = jnp.int32(0)
        for t in range(N_TP):
            rank += jnp.where(t < device, alive[t, replica], 0)
        return alive[device, replica], rank * width

    return width, holds


def selection(width, held, first_wanted):
    is_alive, first_held = held
    wanted = lax.broadcasted_iota(jnp.int32, (COMMON, SLOT), 0)
    cols = lax.broadcasted_iota(jnp.int32, (COMMON, SLOT), 1)
    shift = jnp.where(is_alive == 1, first_wanted - first_held, 4 * FF)
    return ((cols - wanted == shift) & (cols < width)).astype(F32).astype(BF16)


def across(a, b):
    return lax.dot_general(a, b, (((1,), (1,)), ((), ())), preferred_element_type=F32)


def even_odd(me, even, odd):
    return me + jnp.where(me % 2 == 0, even, odd)


def early_kernel(where, alive, own, out, select):
    @pl.when(pl.program_id(0) == 0)
    def _():
        width, holds = layout(where, alive)
        me = where[1]
        select[...] = selection(width, holds(me), even_odd(me, -2, 2) * COMMON)

    out[...] = across(select[...], own[...]).astype(BF16)


def late_kernel(where, alive, own, other, out, select):
    @pl.when(pl.program_id(0) == 0)
    def _():
        width, holds = layout(where, alive)
        me = where[1]
        first = even_odd(me, 2, -2) * COMMON
        select[0] = selection(width, holds(me), first)
        select[1] = selection(width, holds(me ^ 1), first)

    out[...] = (across(select[0], own[...]) + across(select[1], other[...])).astype(BF16)


def hidden_kernel(where, alive, grad, weight, own, other, grad_hidden, grad_t, local, select):
    width, holds = layout(where, alive)
    me = where[1]
    mine = holds(me)

    @pl.when(pl.program_id(0) == 0)
    def _():
        select[0] = selection(width, mine, me * COMMON)
        select[1] = selection(width, holds(me ^ 1), me * COMMON)

    block = grad[...]
    product = across(block, weight[...])
    cols = lax.broadcasted_iota(jnp.int32, product.shape, 1)
    limit = jnp.where(mine[0] == 1, width, 0)
    grad_hidden[...] = jnp.where(cols < limit, product, 0.0).astype(BF16)
    local[...] = (across(select[0], own[...]) + across(select[1], other[...])).astype(BF16)
    grad_t[...] = block.T


def steps_of(most):
    return jnp.ceil(256.0 * (jnp.log2(jnp.maximum(most, 1e-30)) - LOG_LEVELS))


def coded(value, inverse):
    return jnp.round(value * inverse).astype(jnp.int32).astype(I16)


def fold(product):
    groups = [product[:, c * 128 : c * 128 + 128] for c in range(3)]
    last = product[:, 384:]
    return groups + [last[:32] + pltpu.roll(last[32:], 64, 1)]


def tallest(value):
    return jnp.max(jnp.abs(value).reshape(value.shape[0] // 8, 8, 128), axis=0)


def write_code(out, index, blocks, folded, most):
    steps = [steps_of(jnp.max(m, axis=0, keepdims=True)) for m in most]
    inverse = [jnp.exp2(step * (-1.0 / 256.0)) for step in steps]
    for block in range(blocks):
        for (row, rows), inv in zip(GROUPS, inverse):
            r = block * ROWS + row
            out[index, r : r + rows] = coded(folded(r, rows), inv)
    head = jnp.concatenate(steps + [jnp.zeros((PAD - len(steps), 128), F32)], axis=0)
    out[index, blocks * ROWS :] = head.astype(jnp.int32).astype(I16)


def read_steps(got, index, blocks):
    head = got[index, blocks * ROWS :].astype(jnp.int32).astype(F32)
    return jnp.exp2(head * (1.0 / 256.0))


def read_sum(got, sources, steps, r, rows, group):
    value = None
    for k in range(sources):
        term = got[k, r : r + rows].astype(jnp.int32).astype(F32) * steps[k][group : group + 1]
        value = term if value is None else value + term
    return value


def partial_kernel(grad_t, local, early, late, out, common, folded, most):
    step = pl.program_id(0)

    @pl.when(step == 0)
    def _():
        common[:COMMON] = local[...] + early[...] + late[...]
        common[COMMON:] = jnp.zeros((SLOT - COMMON, TOK), BF16)
        most[...] = jnp.zeros(most.shape, F32)

    got = across(grad_t[...], common[...])
    for near in range(NEAR):
        for g, ((row, rows), part) in enumerate(zip(GROUPS, fold(got[near * 64 : near * 64 + 64]))):
            folded[step, near, row : row + rows] = part
            most[near, g] = jnp.maximum(most[near, g], tallest(part))

    @pl.when(step == FAR - 1)
    def _():
        for near in range(NEAR):
            write_code(
                out,
                near,
                FAR,
                lambda r, rows: folded[r // ROWS, near, r % ROWS : r % ROWS + rows],
                [most[near, g] for g in range(len(GROUPS))],
            )


def middle_kernel(got, out, folded):
    steps = [read_steps(got, k, FAR) for k in range(NEAR)]
    for far in range(FAR):
        most = []
        for g, (row, rows) in enumerate(GROUPS):
            value = read_sum(got, NEAR, steps, far * ROWS + row, rows, g)
            folded[row : row + rows] = value
            most.append(tallest(value))
        write_code(out, far, 1, lambda r, rows: folded[r : r + rows], most)


def final_kernel(got, out):
    steps = [read_steps(got, k, 1) * FACTOR for k in range(FAR)]
    parts = [read_sum(got, FAR, steps, row, rows, g) for g, (row, rows) in enumerate(GROUPS)]
    for c in range(3):
        out[:, c * 128 : c * 128 + 128] = parts[c]
    out[:32, 384:] = parts[3][:, :64]
    out[32:, 384:] = pltpu.roll(parts[3], 64, 1)[:, :64]


def shape(dims, kind):
    return jax.ShapeDtypeStruct(dims, kind)


def params(mib):
    return pltpu.CompilerParams(vmem_limit_bytes=mib << 20)


def block(dims, index):
    return pl.BlockSpec(dims, index)


def local(hidden, grad_out, weight, alive):
    where = jnp.stack([lax.axis_index("rep"), lax.axis_index("tp")]).astype(jnp.int32)
    alive = alive.T
    other = lax.ppermute(hidden, "tp", [(t, t ^ 1) for t in range(N_TP)])
    step = 256
    grid = (TOK // step,)
    tokens = block((step, SLOT), lambda i: (i, 0))
    window = block((COMMON, step), lambda i: (0, i))
    early = pl.pallas_call(
        early_kernel,
        grid=grid,
        out_shape=shape((COMMON, TOK), BF16),
        in_specs=[SMEM, SMEM, tokens],
        out_specs=window,
        scratch_shapes=[pltpu.VMEM((COMMON, SLOT), BF16)],
        compiler_params=params(56),
        name="early_window",
    )(where, alive, hidden)
    early = lax.ppermute(early, "tp", [(t, t + 2) for t in range(7, 14, 2)] + [(t, t - 2) for t in range(2, 9, 2)])
    late = pl.pallas_call(
        late_kernel,
        grid=grid,
        out_shape=shape((COMMON, TOK), BF16),
        in_specs=[SMEM, SMEM, tokens, tokens],
        out_specs=window,
        scratch_shapes=[pltpu.VMEM((2, COMMON, SLOT), BF16)],
        compiler_params=params(24),
        name="late_window",
    )(where, alive, hidden, other)
    late = lax.ppermute(late, "tp", [(t, t + 2) for t in range(0, 14, 2)] + [(t, t - 2) for t in range(3, 16, 2)])
    grad_hidden, grad_t, own = pl.pallas_call(
        hidden_kernel,
        grid=grid,
        out_shape=[shape((TOK, SLOT), BF16), shape((D, TOK), BF16), shape((COMMON, TOK), BF16)],
        in_specs=[SMEM, SMEM, block((step, D), lambda i: (i, 0)), block((SLOT, D), lambda i: (0, 0)), tokens, tokens],
        out_specs=[tokens, block((D, step), lambda i: (0, i)), window],
        scratch_shapes=[pltpu.VMEM((2, COMMON, SLOT), BF16)],
        compiler_params=params(28),
        cost_estimate=pl.CostEstimate(flops=2 * TOK * SLOT * (D + 2 * COMMON), bytes_accessed=16 << 20, transcendentals=0),
        name="hidden_grad",
    )(where, alive, grad_out, weight[0], hidden, other)
    whole = block((COMMON, TOK), lambda i: (0, 0))
    payload = pl.pallas_call(
        partial_kernel,
        grid=(FAR,),
        out_shape=shape((NEAR, FAR * ROWS + PAD, 128), I16),
        in_specs=[block((D // FAR, TOK), lambda i: (i, 0)), whole, whole, whole],
        out_specs=block((NEAR, FAR * ROWS + PAD, 128), lambda i: (0, 0, 0)),
        scratch_shapes=[
            pltpu.VMEM((SLOT, TOK), BF16),
            pltpu.VMEM((FAR, NEAR, ROWS, 128), F32),
            pltpu.VMEM((NEAR, len(GROUPS), 8, 128), F32),
        ],
        compiler_params=params(32),
        name="partial",
    )(grad_t, own, early, late)
    payload = lax.all_to_all(
        payload, "rep", 0, 0, axis_index_groups=[[f * NEAR + n for n in range(NEAR)] for f in range(FAR)]
    )
    payload = pl.pallas_call(
        middle_kernel,
        out_shape=shape((FAR, ROWS + PAD, 128), I16),
        in_specs=[VMEM],
        out_specs=VMEM,
        scratch_shapes=[pltpu.VMEM((ROWS, 128), F32)],
        compiler_params=params(16),
        name="middle",
    )(payload)
    payload = lax.all_to_all(
        payload, "rep", 0, 0, axis_index_groups=[[f * NEAR + n for f in range(FAR)] for n in range(NEAR)]
    )
    grad_weight_t = pl.pallas_call(
        final_kernel,
        out_shape=shape((64, COMMON), F32),
        in_specs=[VMEM],
        out_specs=VMEM,
        compiler_params=params(16),
        name="final",
    )(payload)
    return grad_hidden, grad_weight_t.T


def solution(mesh):
    return jax.shard_map(
        local,
        mesh=mesh,
        in_specs=(P("rep", "tp"), P("rep", None), P("rep", "tp", None), P()),
        out_specs=(P("rep", "tp"), P("tp", "rep")),
        check_vma=False,
    )
```

time: 104 us -> 90.3 us (0.87)
  local copies, waits for them, and re-layouts: 17.5 us -> 3.56 us
  waiting for transfers between devices: 13.3 us -> 5.44 us
  Pallas kernels: 13.5 us -> 18.3 us
  blocking collectives: 49.6 us -> 52 us
    unnamed x15 -> x14, local copies, waits for them, and re-layouts: 10.9 us -> 3.56 us
    ppermute x2, waiting for transfers between devices: 11.3 us -> 5.44 us  [the longest x1 5.44 us: local(): lax.ppermute(late, 'tp', [(t, t + 2) for t in range(0, 14, 2)] + [(t, t -...]
    pallas_call x3 -> x4, Pallas kernels: 12.1 us -> 17 us  [the longest x1 6.14 us: local(): pl.pallas_call(hidden_kernel, grid=grid, out_shape=[shape((TOK, SLOT), BF...]
    pallas_call x2 -> x0, local copies, waits for them, and re-layouts: 3.66 us -> none  [local(): pl.pallas_call(windows_kernel, out_shape=[shape((TOK, COMMON), BF16)] * 2...]
    ppermute x2 -> x0, local copies, waits for them, and re-layouts: 2.92 us -> none  [the longest x1 1.46 us: local(): lax.ppermute(left, 'tp', [(t, t - 2) for t in range(2, 16) if t % 2 == 1...]
    all_to_all x2, blocking collectives: 49.6 us -> 52 us  [local(): lax.all_to_all(payload, 'rep', 0, 0, axis_index_groups=[[f * NEAR + n for...]
    ppermute x1, waiting for transfers between devices: 1.98 us -> 0.01 us  [local(): other = lax.ppermute(hidden, 'tp', [(t, t ^ 1) for t in range(N_TP)])]
  transfers between devices with their start and end apart: 3 -> 3, of which waited for: 3 -> 1; matrix products, arithmetic and copies ran while one was open for 3% -> 1% of each run, Pallas kernels for 6% -> 15%
where the time goes in v2:
time: 90.3 us; the launch traced here: 89.9 us
  blocking collectives  52 us (58%)
  Pallas kernels  18.3 us (20%)
  starting transfers between devices  9.15 us (10%)
  waiting for transfers between devices  5.44 us (6%)
  local copies, waits for them, and re-layouts  3.56 us (4%)
    all_to_all x2, blocking collectives, local(): lax.all_to_all(payload, 'rep', 0, 0, axis_index_groups=[[f * NEAR + n for...  52 us
    pallas_call x1, Pallas kernels, local(): pl.pallas_call(hidden_kernel, grid=grid, out_shape=[shape((TOK, SLOT), BF...  6.14 us
    ppermute x1, waiting for transfers between devices, local(): lax.ppermute(late, 'tp', [(t, t + 2) for t in range(0, 14, 2)] + [(t, t -...  5.44 us
    ppermute x1, starting transfers between devices, local(): lax.ppermute(late, 'tp', [(t, t + 2) for t in range(0, 14, 2)] + [(t, t -...  4.75 us
    pallas_call x1, Pallas kernels, local(): pl.pallas_call(early_kernel, grid=grid, out_shape=shape((COMMON, TOK), BF...  4.12 us
    pallas_call x1, Pallas kernels, local(): pl.pallas_call(partial_kernel, grid=(FAR,), out_shape=shape((NEAR, FAR *...  3.88 us
    unnamed x14, local copies, waits for them, and re-layouts  3.56 us
    pallas_call x1, Pallas kernels, local(): pl.pallas_call(late_kernel, grid=grid, out_shape=shape((COMMON, TOK), BF1...  2.84 us
  transfers between devices with their start and end apart: 3, of which 1 were waited for; matrix products, arithmetic and copies ran while one was open for 1% of the time, Pallas kernels for 15%

profile of v2, /device:TPU:24, one launch (start us, length us, event | category | flops | bytes accessed | tf_op | source)
XLA Modules:
  0.0 89.9 jit_solution(17891876260809620139)
XLA Ops:
  0.6 0.0 copy-start
  0.6 2.1 %collective-permute-start = (bf16[1024,512]{1,0:T(8,128)(2,1)}, bf16[1024,512]{1,0:T(8,128)(2,1)S(1)}, u32[]{:S(2)}, u32[]{:S(2)}) collective-permute-start(bf16[1024,512]{1,0:T(8,128)(2,1)} %own.5), channel_id=1, source_target_pairs={{0,1},{1,0},{2,3},{3,2},{4,5},{5,4},{6,7},{7,6},{8,9},{9,8},{10,11... | collective-permute-start | bytes 3145736 | tf_op jit(solution)/shard_map/ppermute | solution.py:201
  2.7 0.6 pad_add_fusion.where
  3.4 0.0 copy-start.2
  3.4 0.0 copy-start.4
  3.4 4.1 %early_window.1 = bf16[448,1024]{1,0:T(8,128)(2,1)} custom-call(s32[2]{0:T(128)} %pad_add_fusion.where, s32[16,32]{1,0:T(8,128)} %bitcast.5, bf16[1024,512]{1,0:T(8,128)(2,1)} %own.5), custom_call_target="tpu_custom_call" | custom-call | tf_op jit(solution)/shard_map/early_window/pallas_call | solution.py:206
  7.5 2.3 %collective-permute-start.1 = (bf16[448,1024]{1,0:T(8,128)(2,1)}, bf16[448,1024]{1,0:T(8,128)(2,1)S(1)}, u32[]{:S(2)}, u32[]{:S(2)}) collective-permute-start(bf16[448,1024]{1,0:T(8,128)(2,1)} %early_window.1), channel_id=1, source_target_pairs={{7,9},{9,11},{11,13},{13,15},{2,0},{4,2},{6,4},{8,6},{23,25},{25,2... | collective-permute-start | bytes 2752520 | tf_op jit(solution)/shard_map/ppermute | solution.py:216
  9.8 0.0 collective-permute-done.other
  9.8 0.0 copy-done
  9.9 0.0 copy-start.1
  9.9 0.7 copy-done.1
  10.6 0.0 copy-start.3
  10.6 0.7 copy-done.3
  11.2 0.0 copy-start.6
  11.2 2.8 %late_window.1 = bf16[448,1024]{1,0:T(8,128)(2,1)S(1)} custom-call(s32[2]{0:T(128)S(1)} %copy-done.3, s32[16,32]{1,0:T(8,128)S(1)} %bitcast.6, bf16[1024,512]{1,0:T(8,128)(2,1)S(1)} %copy-done, bf16[1024,512]{1,0:T(8,128)(2,1)S(1)} %collective-permute-done.other), custom_call_target="tpu_custom_call" | custom-call | tf_op jit(solution)/shard_map/late_window/pallas_call | solution.py:217
  14.1 4.7 %collective-permute-start.2 = (bf16[448,1024]{1,0:T(8,128)(2,1)S(1)}, bf16[448,1024]{1,0:T(8,128)(2,1)S(1)}, u32[]{:S(2)}, u32[]{:S(2)}) collective-permute-start(bf16[448,1024]{1,0:T(8,128)(2,1)S(1)} %late_window.1), channel_id=1, source_target_pairs={{0,2},{2,4},{4,6},{6,8},{8,10},{10,12},{12,14},{3,1},{5,3},{7,5},{... | collective-permute-start | bytes 2752520 | tf_op jit(solution)/shard_map/ppermute | solution.py:227
  18.8 0.0 copy-done.2
  18.8 0.0 copy-done.4
  18.8 0.0 copy-done.6
  18.9 0.0 copy-start.5
  18.9 2.2 %copy-done.5 = bf16[1024,2048]{1,0:T(8,128)(2,1)S(1)} copy-done((bf16[1024,2048]{1,0:T(8,128)(2,1)S(1)}, bf16[1024,2048]{1,0:T(8,128)(2,1)}, u32[]{:S(2)}) %copy-start.5) | copy-done | bytes 4194328
  21.0 6.1 %hidden_grad.1 = (bf16[1024,512]{1,0:T(8,128)(2,1)}, bf16[2048,1024]{1,0:T(8,128)(2,1)S(1)}, bf16[448,1024]{1,0:T(8,128)(2,1)S(1)}) custom-call(s32[2]{0:T(128)S(1)} %copy-done.4, s32[16,32]{1,0:T(8,128)S(1)} %bitcast.7, bf16[1024,2048]{1,0:T(8,128)(2,1)S(1)} %copy-done.5, bf16[512,2048]{1,0:T(8,128)(2,1)S(1)} %bitcast.8, bf16[1024,512]{1,0:T(8,128)(2,1)S(1)} %copy-done, ...), custom_call_target="tpu_custom_call" | custom-call | flops 3087007744 | bytes 16777216 | tf_op jit(solution)/shard_map/hidden_grad/pallas_call | solution.py:228
  27.2 0.0 collective-permute-done.1.early
  27.2 5.4 %collective-permute-done.2.late = bf16[448,1024]{1,0:T(8,128)(2,1)S(1)} collective-permute-done((bf16[448,1024]{1,0:T(8,128)(2,1)S(1)}, bf16[448,1024]{1,0:T(8,128)(2,1)S(1)}, u32[]{:S(2)}, u32[]{:S(2)}) %collective-permute-start.2) | collective-permute-done | bytes 917536 | tf_op jit(solution)/shard_map/ppermute | solution.py:227
  32.6 3.9 %partial.1 = s16[8,912,128]{2,1,0:T(8,128)(2,1)S(1)} custom-call(bf16[2048,1024]{1,0:T(8,128)(2,1)S(1)} %get-tuple-element.6.grad_t, bf16[448,1024]{1,0:T(8,128)(2,1)S(1)} %get-tuple-element.7.local, bf16[448,1024]{1,0:T(8,128)(2,1)S(1)} %collective-permute-done.1.early, bf16[448,1024]{1,0:T(8,128)(2,1)S(1)} %collective-permute-done.2.late), custom_call_target="tpu_custom_call" | custom-call | tf_op jit(solution)/shard_map/partial/pallas_call | solution.py:240
  36.5 32.2 %all_to_all.10.got = s16[8,912,128]{2,1,0:T(8,128)(2,1)S(1)} all-to-all(s16[8,912,128]{2,1,0:T(8,128)(2,1)S(1)} %partial.1), channel_id=1, replica_groups={{0,16,32,48,64,80,96,112},{128,144,160,176,192,208,224,240},{256,272,28..., dimensions={0} | all-to-all | bytes 3735552 | tf_op jit(solution)/shard_map/all_to_all | solution.py:254
  68.7 0.6 middle.1
  69.3 19.8 %all_to_all.11.got = s16[4,240,128]{2,1,0:T(8,128)(2,1)S(1)} all-to-all(s16[4,240,128]{2,1,0:T(8,128)(2,1)S(1)} %middle.1), channel_id=1, replica_groups={{0,128,256,384},{16,144,272,400},{32,160,288,416},{48,176,304,432},{64,..., dimensions={0} | all-to-all | bytes 491520 | tf_op jit(solution)/shard_map/all_to_all | solution.py:266
  89.1 0.8 final.1
Async XLA Ops:
  0.6 9.2 %copy-start = (bf16[1024,512]{1,0:T(8,128)(2,1)S(1)}, bf16[1024,512]{1,0:T(8,128)(2,1)}, u32[]{:S(2)}) copy-start(bf16[1024,512]{1,0:T(8,128)(2,1)} %own.5) | copy-start | bytes 3145732
  0.6 9.2 %collective-permute-start = (bf16[1024,512]{1,0:T(8,128)(2,1)}, bf16[1024,512]{1,0:T(8,128)(2,1)S(1)}, u32[]{:S(2)}, u32[]{:S(2)}) collective-permute-start(bf16[1024,512]{1,0:T(8,128)(2,1)} %own.5), channel_id=1, source_target_pairs={{0,1},{1,0},{2,3},{3,2},{4,5},{5,4},{6,7},{7,6},{8,9},{9,8},{10,11... | collective-permute-start | bytes 3145736 | tf_op jit(solution)/shard_map/ppermute | solution.py:201
  3.4 15.5 %copy-start.2 = (s32[32,16]{0,1:T(8,128)S(1)}, s32[32,16]{0,1:T(8,128)}, u32[]{:S(2)}) copy-start(s32[32,16]{0,1:T(8,128)} %param.7) | copy-start | bytes 6148
  3.4 15.5 %copy-start.4 = (s32[2]{0:T(128)S(1)}, s32[2]{0:T(128)}, u32[]{:S(2)}) copy-start(s32[2]{0:T(128)} %pad_add_fusion.where) | copy-start | bytes 28
  7.5 19.7 %collective-permute-start.1 = (bf16[448,1024]{1,0:T(8,128)(2,1)}, bf16[448,1024]{1,0:T(8,128)(2,1)S(1)}, u32[]{:S(2)}, u32[]{:S(2)}) collective-permute-start(bf16[448,1024]{1,0:T(8,128)(2,1)} %early_window.1), channel_id=1, source_target_pairs={{7,9},{9,11},{11,13},{13,15},{2,0},{4,2},{6,4},{8,6},{23,25},{25,2... | collective-permute-start | bytes 2752520 | tf_op jit(solution)/shard_map/ppermute | solution.py:216
  9.9 0.7 copy-start.1
  10.6 0.7 copy-start.3
  11.2 7.6 %copy-start.6 = (bf16[1,512,2048]{2,1,0:T(8,128)(2,1)S(1)}, bf16[1,512,2048]{2,1,0:T(8,128)(2,1)}, u32[]{:S(2)}) copy-start(bf16[1,512,2048]{2,1,0:T(8,128)(2,1)} %param.6) | copy-start | bytes 6291460
  14.1 18.6 %collective-permute-start.2 = (bf16[448,1024]{1,0:T(8,128)(2,1)S(1)}, bf16[448,1024]{1,0:T(8,128)(2,1)S(1)}, u32[]{:S(2)}, u32[]{:S(2)}) collective-permute-start(bf16[448,1024]{1,0:T(8,128)(2,1)S(1)} %late_window.1), channel_id=1, source_target_pairs={{0,2},{2,4},{4,6},{6,8},{8,10},{10,12},{12,14},{3,1},{5,3},{7,5},{... | collective-permute-start | bytes 2752520 | tf_op jit(solution)/shard_map/ppermute | solution.py:227
  18.9 2.2 %copy-start.5 = (bf16[1024,2048]{1,0:T(8,128)(2,1)S(1)}, bf16[1024,2048]{1,0:T(8,128)(2,1)}, u32[]{:S(2)}) copy-start(bf16[1024,2048]{1,0:T(8,128)(2,1)} %grad.1) | copy-start | bytes 12582916

commit v3 on v2

--- a/solution.py
+++ b/solution.py
@@ -53,14 +53,11 @@
     return me + jnp.where(me % 2 == 0, even, odd)
 
 
-def early_kernel(where, alive, own, out, select):
-    @pl.when(pl.program_id(0) == 0)
-    def _():
-        width, holds = layout(where, alive)
-        me = where[1]
-        select[...] = selection(width, holds(me), even_odd(me, -2, 2) * COMMON)
-
-    out[...] = across(select[...], own[...]).astype(BF16)
+def merge_kernel(where, alive, local, early, out):
+    width, holds = layout(where, alive)
+    me = where[1]
+    source = jnp.clip(even_odd(me, 2, -2), 0, N_TP - 1)
+    out[...] = local[...] + across(selection(width, holds(source), me * COMMON), early[...]).astype(BF16)
 
 
 def late_kernel(where, alive, own, other, out, select):
@@ -136,31 +133,22 @@
     return value
 
 
-def partial_kernel(grad_t, local, early, late, out, common, folded, most):
-    step = pl.program_id(0)
-
-    @pl.when(step == 0)
-    def _():
-        common[:COMMON] = local[...] + early[...] + late[...]
-        common[COMMON:] = jnp.zeros((SLOT - COMMON, TOK), BF16)
-        most[...] = jnp.zeros(most.shape, F32)
-
-    got = across(grad_t[...], common[...])
+def partial_kernel(grad_t, local, late, out, common, folded):
+    common[:COMMON] = local[...] + late[...]
+    common[COMMON:] = jnp.zeros((SLOT - COMMON, TOK), BF16)
+    most = [[None] * len(GROUPS) for _ in range(NEAR)]
+    step = 256
+    for f in range(0, D, step):
+        got = across(grad_t[f : f + step], common[...])
+        for owner in range(f // 64, (f + step) // 64):
+            far, near = owner // NEAR, owner % NEAR
+            parts = fold(got[owner * 64 - f : owner * 64 - f + 64])
+            for g, ((row, rows), part) in enumerate(zip(GROUPS, parts)):
+                folded[near, far * ROWS + row : far * ROWS + row + rows] = part
+                big = tallest(part)
+                most[near][g] = big if far == 0 else jnp.maximum(most[near][g], big)
     for near in range(NEAR):
-        for g, ((row, rows), part) in enumerate(zip(GROUPS, fold(got[near * 64 : near * 64 + 64]))):
-            folded[step, near, row : row + rows] = part
-            most[near, g] = jnp.maximum(most[near, g], tallest(part))
-
-    @pl.when(step == FAR - 1)
-    def _():
-        for near in range(NEAR):
-            write_code(
-                out,
-                near,
-                FAR,
-                lambda r, rows: folded[r // ROWS, near, r % ROWS : r % ROWS + rows],
-                [most[near, g] for g in range(len(GROUPS))],
-            )
+        write_code(out, near, FAR, lambda r, rows: folded[near, r : r + rows], most[near])
 
 
 def middle_kernel(got, out, folded):
@@ -203,17 +191,7 @@
     grid = (TOK // step,)
     tokens = block((step, SLOT), lambda i: (i, 0))
     window = block((COMMON, step), lambda i: (0, i))
-    early = pl.pallas_call(
-        early_kernel,
-        grid=grid,
-        out_shape=shape((COMMON, TOK), BF16),
-        in_specs=[SMEM, SMEM, tokens],
-        out_specs=window,
-        scratch_shapes=[pltpu.VMEM((COMMON, SLOT), BF16)],
-        compiler_params=params(56),
-        name="early_window",
-    )(where, alive, hidden)
-    early = lax.ppermute(early, "tp", [(t, t + 2) for t in range(7, 14, 2)] + [(t, t - 2) for t in range(2, 9, 2)])
+    early = lax.ppermute(hidden, "tp", [(t, t + 2) for t in range(7, 14, 2)] + [(t, t - 2) for t in range(2, 9, 2)])
     late = pl.pallas_call(
         late_kernel,
         grid=grid,
@@ -236,21 +214,23 @@
         cost_estimate=pl.CostEstimate(flops=2 * TOK * SLOT * (D + 2 * COMMON), bytes_accessed=16 << 20, transcendentals=0),
         name="hidden_grad",
     )(where, alive, grad_out, weight[0], hidden, other)
-    whole = block((COMMON, TOK), lambda i: (0, 0))
+    own = pl.pallas_call(
+        merge_kernel,
+        out_shape=shape((COMMON, TOK), BF16),
+        in_specs=[SMEM, SMEM, VMEM, VMEM],
+        out_specs=VMEM,
+        compiler_params=params(24),
+        name="merge",
+    )(where, alive, own, early)
     payload = pl.pallas_call(
         partial_kernel,
-        grid=(FAR,),
         out_shape=shape((NEAR, FAR * ROWS + PAD, 128), I16),
-        in_specs=[block((D // FAR, TOK), lambda i: (i, 0)), whole, whole, whole],
-        out_specs=block((NEAR, FAR * ROWS + PAD, 128), lambda i: (0, 0, 0)),
-        scratch_shapes=[
-            pltpu.VMEM((SLOT, TOK), BF16),
-            pltpu.VMEM((FAR, NEAR, ROWS, 128), F32),
-            pltpu.VMEM((NEAR, len(GROUPS), 8, 128), F32),
-        ],
+        in_specs=[VMEM] * 3,
+        out_specs=VMEM,
+        scratch_shapes=[pltpu.VMEM((SLOT, TOK), BF16), pltpu.VMEM((NEAR, FAR * ROWS, 128), F32)],
         compiler_params=params(32),
         name="partial",
-    )(grad_t, own, early, late)
+    )(grad_t, own, late)
     payload = lax.all_to_all(
         payload, "rep", 0, 0, axis_index_groups=[[f * NEAR + n for n in range(NEAR)] for f in range(FAR)]
     )

time: 90.3 us -> 85.7 us (0.949)
  Pallas kernels: 18.3 us -> 14.5 us
  local copies, waits for them, and re-layouts: 3.56 us -> 5.7 us
  waiting for transfers between devices: 5.44 us -> 3.33 us
    pallas_call x2, Pallas kernels: 8 us -> 4.22 us  [the longest x1 2.83 us: local(): pl.pallas_call(partial_kernel, out_shape=shape((NEAR, FAR * ROWS + PAD, 1...]
    ppermute x1, waiting for transfers between devices: 5.44 us -> 2.94 us  [local(): lax.ppermute(late, 'tp', [(t, t + 2) for t in range(0, 14, 2)] + [(t, t -...]
    unnamed x14 -> x12, local copies, waits for them, and re-layouts: 3.56 us -> 5.7 us
  transfers between devices with their start and end apart: 3 -> 3, of which waited for: 1 -> 2; matrix products, arithmetic and copies ran while one was open for 1% -> 0% of each run, Pallas kernels for 15% -> 12%
where the time goes in v3:
time: 85.7 us; the launch traced here: 85.3 us
  blocking collectives  51.9 us (61%)
  Pallas kernels  14.5 us (17%)
  starting transfers between devices  8.97 us (10%)
  local copies, waits for them, and re-layouts  5.7 us (7%)
  waiting for transfers between devices  3.33 us (4%)
    all_to_all x2, blocking collectives, local(): lax.all_to_all(payload, 'rep', 0, 0, axis_index_groups=[[f * NEAR + n for...  51.9 us
    pallas_call x1, Pallas kernels, local(): pl.pallas_call(hidden_kernel, grid=grid, out_shape=[shape((TOK, SLOT), BF...  6.12 us
    unnamed x12, local copies, waits for them, and re-layouts  5.7 us
    ppermute x1, starting transfers between devices, local(): lax.ppermute(late, 'tp', [(t, t + 2) for t in range(0, 14, 2)] + [(t, t -...  4.69 us
    ppermute x1, waiting for transfers between devices, local(): lax.ppermute(late, 'tp', [(t, t + 2) for t in range(0, 14, 2)] + [(t, t -...  2.94 us
    pallas_call x1, Pallas kernels, local(): pl.pallas_call(late_kernel, grid=grid, out_shape=shape((COMMON, TOK), BF1...  2.84 us
    pallas_call x1, Pallas kernels, local(): pl.pallas_call(partial_kernel, out_shape=shape((NEAR, FAR * ROWS + PAD, 1...  2.83 us
    ppermute x1, starting transfers between devices, local(): lax.ppermute(hidden, 'tp', [(t, t + 2) for t in range(7, 14, 2)] + [(t, t...  2.36 us
  transfers between devices with their start and end apart: 3, of which 2 were waited for; matrix products, arithmetic and copies ran while one was open for 0% of the time, Pallas kernels for 12%

profile of v3, /device:TPU:24, one launch (start us, length us, event | category | flops | bytes accessed | tf_op | source)
XLA Modules:
  0.0 85.3 jit_solution(14030602913873523990)
XLA Ops:
  0.6 0.0 copy-start.3
  0.6 1.9 %collective-permute-start = (bf16[1024,512]{1,0:T(8,128)(2,1)}, bf16[1024,512]{1,0:T(8,128)(2,1)S(1)}, u32[]{:S(2)}, u32[]{:S(2)}) collective-permute-start(bf16[1024,512]{1,0:T(8,128)(2,1)} %own.3), channel_id=1, source_target_pairs={{0,1},{1,0},{2,3},{3,2},{4,5},{5,4},{6,7},{7,6},{8,9},{9,8},{10,11... | collective-permute-start | bytes 3145736 | tf_op jit(solution)/shard_map/ppermute | solution.py:189
  2.6 2.4 %collective-permute-start.1 = (bf16[1024,512]{1,0:T(8,128)(2,1)}, bf16[1024,512]{1,0:T(8,128)(2,1)S(1)}, u32[]{:S(2)}, u32[]{:S(2)}) collective-permute-start(bf16[1024,512]{1,0:T(8,128)(2,1)} %own.3), channel_id=1, source_target_pairs={{7,9},{9,11},{11,13},{13,15},{2,0},{4,2},{6,4},{8,6},{23,25},{25,2... | collective-permute-start | bytes 3145736 | tf_op jit(solution)/shard_map/ppermute | solution.py:194
  4.9 0.1 pad_add_fusion.where
  5.0 0.4 collective-permute-done.other
  5.4 0.0 copy-start
  5.4 1.2 %copy-done = bf16[1024,512]{1,0:T(8,128)(2,1)S(1)} copy-done((bf16[1024,512]{1,0:T(8,128)(2,1)S(1)}, bf16[1024,512]{1,0:T(8,128)(2,1)}, u32[]{:S(2)}) %copy-start) | copy-done | bytes 1048600
  6.6 0.0 copy-start.2
  6.6 0.7 copy-done.2
  7.3 0.0 copy-start.1
  7.3 2.8 %late_window.1 = bf16[448,1024]{1,0:T(8,128)(2,1)S(1)} custom-call(s32[2]{0:T(128)S(1)} %pad_add_fusion.where, s32[16,32]{1,0:T(8,128)S(1)} %bitcast.5, bf16[1024,512]{1,0:T(8,128)(2,1)S(1)} %copy-done, bf16[1024,512]{1,0:T(8,128)(2,1)S(1)} %collective-permute-done.other), custom_call_target="tpu_custom_call" | custom-call | tf_op jit(solution)/shard_map/late_window/pallas_call | solution.py:195
  10.2 4.7 %collective-permute-start.2 = (bf16[448,1024]{1,0:T(8,128)(2,1)S(1)}, bf16[448,1024]{1,0:T(8,128)(2,1)S(1)}, u32[]{:S(2)}, u32[]{:S(2)}) collective-permute-start(bf16[448,1024]{1,0:T(8,128)(2,1)S(1)} %late_window.1), channel_id=1, source_target_pairs={{0,2},{2,4},{4,6},{6,8},{8,10},{10,12},{12,14},{3,1},{5,3},{7,5},{... | collective-permute-start | bytes 2752520 | tf_op jit(solution)/shard_map/ppermute | solution.py:205
  14.9 0.0 copy-done.3
  14.9 0.0 copy-done.1
  14.9 0.0 copy-start.4
  14.9 2.2 %copy-done.4 = bf16[1024,2048]{1,0:T(8,128)(2,1)S(1)} copy-done((bf16[1024,2048]{1,0:T(8,128)(2,1)S(1)}, bf16[1024,2048]{1,0:T(8,128)(2,1)}, u32[]{:S(2)}) %copy-start.4) | copy-done | bytes 4194328
  17.1 0.0 copy-start.5
  17.1 1.6 %copy-done.5 = bf16[1,512,2048]{2,1,0:T(8,128)(2,1)S(1)} copy-done((bf16[1,512,2048]{2,1,0:T(8,128)(2,1)S(1)}, bf16[1,512,2048]{2,1,0:T(8,128)(2,1)}, u32[]{:S(2)}) %copy-start.5) | copy-done | bytes 2097176
  18.7 6.1 %hidden_grad.1 = (bf16[1024,512]{1,0:T(8,128)(2,1)}, bf16[2048,1024]{1,0:T(8,128)(2,1)S(1)}, bf16[448,1024]{1,0:T(8,128)(2,1)S(1)}) custom-call(s32[2]{0:T(128)S(1)} %pad_add_fusion.where, s32[16,32]{1,0:T(8,128)S(1)} %bitcast.6, bf16[1024,2048]{1,0:T(8,128)(2,1)S(1)} %copy-done.4, bf16[512,2048]{1,0:T(8,128)(2,1)S(1)} %bitcast.8, ...), custom_call_target="tpu_custom_call" | custom-call | flops 3087007744 | bytes 16777216 | tf_op jit(solution)/shard_map/hidden_grad/pallas_call | solution.py:206
  24.8 0.0 collective-permute-done.1.early
  24.8 1.4 %merge.1.local = bf16[448,1024]{1,0:T(8,128)(2,1)S(1)} custom-call(s32[2]{0:T(128)S(1)} %pad_add_fusion.where, s32[16,32]{1,0:T(8,128)S(1)} %bitcast.7, bf16[448,1024]{1,0:T(8,128)(2,1)S(1)} %get-tuple-element.7.local, bf16[1024,512]{1,0:T(8,128)(2,1)S(1)} %collective-permute-done.1.early), custom_call_target="tpu_custom_call" | custom-call | tf_op jit(solution)/shard_map/merge/pallas_call | solution.py:217
  26.2 2.9 %collective-permute-done.2.late = bf16[448,1024]{1,0:T(8,128)(2,1)S(1)} collective-permute-done((bf16[448,1024]{1,0:T(8,128)(2,1)S(1)}, bf16[448,1024]{1,0:T(8,128)(2,1)S(1)}, u32[]{:S(2)}, u32[]{:S(2)}) %collective-permute-start.2) | collective-permute-done | bytes 917536 | tf_op jit(solution)/shard_map/ppermute | solution.py:205
  29.1 2.8 %partial.1 = s16[8,912,128]{2,1,0:T(8,128)(2,1)S(1)} custom-call(bf16[2048,1024]{1,0:T(8,128)(2,1)S(1)} %get-tuple-element.6.grad_t, bf16[448,1024]{1,0:T(8,128)(2,1)S(1)} %merge.1.local, bf16[448,1024]{1,0:T(8,128)(2,1)S(1)} %collective-permute-done.2.late), custom_call_target="tpu_custom_call" | custom-call | tf_op jit(solution)/shard_map/partial/pallas_call | solution.py:225
  32.0 32.2 %all_to_all.10.got = s16[8,912,128]{2,1,0:T(8,128)(2,1)S(1)} all-to-all(s16[8,912,128]{2,1,0:T(8,128)(2,1)S(1)} %partial.1), channel_id=1, replica_groups={{0,16,32,48,64,80,96,112},{128,144,160,176,192,208,224,240},{256,272,28..., dimensions={0} | all-to-all | bytes 3735552 | tf_op jit(solution)/shard_map/all_to_all | solution.py:234
  64.2 0.6 middle.1
  64.7 19.8 %all_to_all.11.got = s16[4,240,128]{2,1,0:T(8,128)(2,1)S(1)} all-to-all(s16[4,240,128]{2,1,0:T(8,128)(2,1)S(1)} %middle.1), channel_id=1, replica_groups={{0,128,256,384},{16,144,272,400},{32,160,288,416},{48,176,304,432},{64,..., dimensions={0} | all-to-all | bytes 491520 | tf_op jit(solution)/shard_map/all_to_all | solution.py:246
  84.5 0.8 final.1
Async XLA Ops:
  0.6 14.3 %copy-start.3 = (s32[32,16]{0,1:T(8,128)S(1)}, s32[32,16]{0,1:T(8,128)}, u32[]{:S(2)}) copy-start(s32[32,16]{0,1:T(8,128)} %param.7) | copy-start | bytes 6148
  0.6 4.8 %collective-permute-start = (bf16[1024,512]{1,0:T(8,128)(2,1)}, bf16[1024,512]{1,0:T(8,128)(2,1)S(1)}, u32[]{:S(2)}, u32[]{:S(2)}) collective-permute-start(bf16[1024,512]{1,0:T(8,128)(2,1)} %own.3), channel_id=1, source_target_pairs={{0,1},{1,0},{2,3},{3,2},{4,5},{5,4},{6,7},{7,6},{8,9},{9,8},{10,11... | collective-permute-start | bytes 3145736 | tf_op jit(solution)/shard_map/ppermute | solution.py:189
  2.6 22.2 %collective-permute-start.1 = (bf16[1024,512]{1,0:T(8,128)(2,1)}, bf16[1024,512]{1,0:T(8,128)(2,1)S(1)}, u32[]{:S(2)}, u32[]{:S(2)}) collective-permute-start(bf16[1024,512]{1,0:T(8,128)(2,1)} %own.3), channel_id=1, source_target_pairs={{7,9},{9,11},{11,13},{13,15},{2,0},{4,2},{6,4},{8,6},{23,25},{25,2... | collective-permute-start | bytes 3145736 | tf_op jit(solution)/shard_map/ppermute | solution.py:194
  5.4 1.2 %copy-start = (bf16[1024,512]{1,0:T(8,128)(2,1)S(1)}, bf16[1024,512]{1,0:T(8,128)(2,1)}, u32[]{:S(2)}) copy-start(bf16[1024,512]{1,0:T(8,128)(2,1)} %own.3) | copy-start | bytes 3145732
  6.6 0.7 copy-start.2
  7.3 7.6 %copy-start.1 = (bf16[1024,512]{1,0:T(8,128)(2,1)S(1)}, bf16[1024,512]{1,0:T(8,128)(2,1)}, u32[]{:S(2)}) copy-start(bf16[1024,512]{1,0:T(8,128)(2,1)} %own.3) | copy-start | bytes 3145732
  10.2 19.0 %collective-permute-start.2 = (bf16[448,1024]{1,0:T(8,128)(2,1)S(1)}, bf16[448,1024]{1,0:T(8,128)(2,1)S(1)}, u32[]{:S(2)}, u32[]{:S(2)}) collective-permute-start(bf16[448,1024]{1,0:T(8,128)(2,1)S(1)} %late_window.1), channel_id=1, source_target_pairs={{0,2},{2,4},{4,6},{6,8},{8,10},{10,12},{12,14},{3,1},{5,3},{7,5},{... | collective-permute-start | bytes 2752520 | tf_op jit(solution)/shard_map/ppermute | solution.py:205
  14.9 2.2 %copy-start.4 = (bf16[1024,2048]{1,0:T(8,128)(2,1)S(1)}, bf16[1024,2048]{1,0:T(8,128)(2,1)}, u32[]{:S(2)}) copy-start(bf16[1024,2048]{1,0:T(8,128)(2,1)} %grad.1) | copy-start | bytes 12582916
  17.1 1.6 %copy-start.5 = (bf16[1,512,2048]{2,1,0:T(8,128)(2,1)S(1)}, bf16[1,512,2048]{2,1,0:T(8,128)(2,1)}, u32[]{:S(2)}) copy-start(bf16[1,512,2048]{2,1,0:T(8,128)(2,1)} %param.6) | copy-start | bytes 6291460

commit v4 on v3

--- a/solution.py
+++ b/solution.py
@@ -15,34 +15,45 @@
 GROUPS = ((0, 64), (64, 64), (128, 64), (192, 32))
 PAD = 16
 LOG_LEVELS = 14.999
+MID = 64
+WIDTH, LIMIT, LATE_OWN, LATE_OTHER, LOCAL_OWN, LOCAL_OTHER, EARLY, MIDDLE, ODD = range(9)
 FACTOR = float(N_REP * TOK) ** -0.5
 F32, BF16, I16 = jnp.float32, jnp.bfloat16, jnp.int16
 VMEM = pl.BlockSpec(memory_space=pltpu.VMEM)
 SMEM = pl.BlockSpec(memory_space=pltpu.SMEM)
 
 
-def layout(where, alive):
-    replica = where[0]
+def plan_kernel(alive, plan):
+    replica, me = lax.axis_index("rep"), lax.axis_index("tp")
     live = jnp.int32(0)
     for t in range(N_TP):
         live += alive[t, replica]
     width = lax.div(jnp.int32(FF), live)
 
-    def holds(device):
+    def shift(device, slot):
         rank = jnp.int32(0)
         for t in range(N_TP):
             rank += jnp.where(t < device, alive[t, replica], 0)
-        return alive[device, replica], rank * width
-
-    return width, holds
-
-
-def selection(width, held, first_wanted):
-    is_alive, first_held = held
-    wanted = lax.broadcasted_iota(jnp.int32, (COMMON, SLOT), 0)
-    cols = lax.broadcasted_iota(jnp.int32, (COMMON, SLOT), 1)
-    shift = jnp.where(is_alive == 1, first_wanted - first_held, 4 * FF)
-    return ((cols - wanted == shift) & (cols < width)).astype(F32).astype(BF16)
+        return jnp.where(alive[device, replica] == 1, slot * COMMON - rank * width, 4 * FF)
+
+    other = me ^ 1
+    back = even_odd(me, -2, 2)
+    away = even_odd(me, 2, -2)
+    plan[WIDTH] = width
+    plan[LIMIT] = jnp.where(alive[me, replica] == 1, width, 0)
+    plan[LATE_OWN] = shift(me, away)
+    plan[LATE_OTHER] = shift(other, away)
+    plan[LOCAL_OWN] = shift(me, me)
+    plan[LOCAL_OTHER] = shift(other, me)
+    plan[EARLY] = shift(jnp.clip(away, 0, N_TP - 1), me)
+    plan[MIDDLE] = shift(me, back) + jnp.where(me % 2 == 0, COMMON - MID, 0)
+    plan[ODD] = me % 2
+
+
+def selection(width, shift, wanted=COMMON):
+    ahead = lax.broadcasted_iota(jnp.int32, (wanted, SLOT), 1) - lax.broadcasted_iota(jnp.int32, (wanted, SLOT), 0)
+    cols = lax.broadcasted_iota(jnp.int32, (wanted, SLOT), 1)
+    return ((ahead == shift) & (cols < width)).astype(F32).astype(BF16)
 
 
 def across(a, b):
@@ -53,42 +64,47 @@
     return me + jnp.where(me % 2 == 0, even, odd)
 
 
-def merge_kernel(where, alive, local, early, out):
-    width, holds = layout(where, alive)
-    me = where[1]
-    source = jnp.clip(even_odd(me, 2, -2), 0, N_TP - 1)
-    out[...] = local[...] + across(selection(width, holds(source), me * COMMON), early[...]).astype(BF16)
-
-
-def late_kernel(where, alive, own, other, out, select):
+def late_kernel(plan, hidden, other, out, middle, own, sem):
+    copy = pltpu.make_async_copy(hidden, own, sem)
+    copy.start()
+    width = plan[WIDTH]
+    from_other = selection(width, plan[LATE_OTHER])
+    from_own = selection(width, plan[LATE_OWN])
+    from_middle = selection(width, plan[MIDDLE], MID)
+    copy.wait()
+    for i in range(0, TOK, 256):
+        got = across(from_own, own[i : i + 256]) + across(from_other, other[i : i + 256])
+        out[:, i : i + 256] = got.astype(BF16)
+        middle[:, i : i + 256] = across(from_middle, own[i : i + 256]).astype(BF16)
+
+
+def merge_kernel(plan, local, early, middle, out):
+    out[...] = local[...] + across(selection(plan[WIDTH], plan[EARLY]), early[...]).astype(BF16)
+
+    @pl.when(plan[ODD] == 1)
+    def _():
+        out[:MID] = out[:MID] + middle[...]
+
+    @pl.when(plan[ODD] == 0)
+    def _():
+        out[COMMON - MID :] = out[COMMON - MID :] + middle[...]
+
+
+def hidden_kernel(plan, grad, weight, own, other, grad_hidden, grad_t, local, select):
     @pl.when(pl.program_id(0) == 0)
     def _():
-        width, holds = layout(where, alive)
-        me = where[1]
-        first = even_odd(me, 2, -2) * COMMON
-        select[0] = selection(width, holds(me), first)
-        select[1] = selection(width, holds(me ^ 1), first)
-
-    out[...] = (across(select[0], own[...]) + across(select[1], other[...])).astype(BF16)
-
-
-def hidden_kernel(where, alive, grad, weight, own, other, grad_hidden, grad_t, local, select):
-    width, holds = layout(where, alive)
-    me = where[1]
-    mine = holds(me)
-
-    @pl.when(pl.program_id(0) == 0)
-    def _():
-        select[0] = selection(width, mine, me * COMMON)
-        select[1] = selection(width, holds(me ^ 1), me * COMMON)
+        select[0] = selection(plan[WIDTH], plan[LOCAL_OWN])
+        select[1] = selection(plan[WIDTH], plan[LOCAL_OTHER])
 
     block = grad[...]
     product = across(block, weight[...])
     cols = lax.broadcasted_iota(jnp.int32, product.shape, 1)
-    limit = jnp.where(mine[0] == 1, width, 0)
-    grad_hidden[...] = jnp.where(cols < limit, product, 0.0).astype(BF16)
+    grad_hidden[...] = jnp.where(cols < plan[LIMIT], product, 0.0).astype(BF16)
     local[...] = (across(select[0], own[...]) + across(select[1], other[...])).astype(BF16)
-    grad_t[...] = block.T
+    turned = block.T
+    for owner in range(N_REP):
+        row = (owner % NEAR * FAR + owner // NEAR) * 64
+        grad_t[row : row + 64] = turned[owner * 64 : owner * 64 + 64]
 
 
 def steps_of(most):
@@ -136,19 +152,16 @@
 def partial_kernel(grad_t, local, late, out, common, folded):
     common[:COMMON] = local[...] + late[...]
     common[COMMON:] = jnp.zeros((SLOT - COMMON, TOK), BF16)
-    most = [[None] * len(GROUPS) for _ in range(NEAR)]
-    step = 256
-    for f in range(0, D, step):
-        got = across(grad_t[f : f + step], common[...])
-        for owner in range(f // 64, (f + step) // 64):
-            far, near = owner // NEAR, owner % NEAR
-            parts = fold(got[owner * 64 - f : owner * 64 - f + 64])
-            for g, ((row, rows), part) in enumerate(zip(GROUPS, parts)):
+    step = FAR * 64
+    for near in range(NEAR):
+        got = across(grad_t[near * step : near * step + step], common[...])
+        most = [None] * len(GROUPS)
+        for far in range(FAR):
+            for g, ((row, rows), part) in enumerate(zip(GROUPS, fold(got[far * 64 : far * 64 + 64]))):
                 folded[near, far * ROWS + row : far * ROWS + row + rows] = part
                 big = tallest(part)
-                most[near][g] = big if far == 0 else jnp.maximum(most[near][g], big)
-    for near in range(NEAR):
-        write_code(out, near, FAR, lambda r, rows: folded[near, r : r + rows], most[near])
+                most[g] = big if far == 0 else jnp.maximum(most[g], big)
+        write_code(out, near, FAR, lambda r, rows: folded[near, r : r + rows], most)
 
 
 def middle_kernel(got, out, folded):
@@ -184,44 +197,47 @@
 
 
 def local(hidden, grad_out, weight, alive):
-    where = jnp.stack([lax.axis_index("rep"), lax.axis_index("tp")]).astype(jnp.int32)
-    alive = alive.T
     other = lax.ppermute(hidden, "tp", [(t, t ^ 1) for t in range(N_TP)])
-    step = 256
-    grid = (TOK // step,)
-    tokens = block((step, SLOT), lambda i: (i, 0))
-    window = block((COMMON, step), lambda i: (0, i))
-    early = lax.ppermute(hidden, "tp", [(t, t + 2) for t in range(7, 14, 2)] + [(t, t - 2) for t in range(2, 9, 2)])
-    late = pl.pallas_call(
+    early = lax.ppermute(hidden, "tp", [(t, t + 2) for t in (9, 11, 13)] + [(t, t - 2) for t in (2, 4, 6)])
+    plan = pl.pallas_call(
+        plan_kernel,
+        out_shape=shape((16,), jnp.int32),
+        in_specs=[SMEM],
+        out_specs=SMEM,
+        name="plan",
+    )(alive.T)
+    late, middle = pl.pallas_call(
         late_kernel,
-        grid=grid,
-        out_shape=shape((COMMON, TOK), BF16),
-        in_specs=[SMEM, SMEM, tokens, tokens],
-        out_specs=window,
-        scratch_shapes=[pltpu.VMEM((2, COMMON, SLOT), BF16)],
+        out_shape=[shape((COMMON, TOK), BF16), shape((MID, TOK), BF16)],
+        in_specs=[SMEM, pl.BlockSpec(memory_space=pltpu.HBM), VMEM],
+        out_specs=[VMEM, VMEM],
+        scratch_shapes=[pltpu.VMEM((TOK, SLOT), BF16), pltpu.SemaphoreType.DMA],
         compiler_params=params(24),
         name="late_window",
-    )(where, alive, hidden, other)
+    )(plan, hidden, other)
     late = lax.ppermute(late, "tp", [(t, t + 2) for t in range(0, 14, 2)] + [(t, t - 2) for t in range(3, 16, 2)])
+    middle = lax.ppermute(middle, "tp", [(7, 9), (8, 6)])
+    step = 256
+    tokens = block((step, SLOT), lambda i: (i, 0))
     grad_hidden, grad_t, own = pl.pallas_call(
         hidden_kernel,
-        grid=grid,
+        grid=(TOK // step,),
         out_shape=[shape((TOK, SLOT), BF16), shape((D, TOK), BF16), shape((COMMON, TOK), BF16)],
-        in_specs=[SMEM, SMEM, block((step, D), lambda i: (i, 0)), block((SLOT, D), lambda i: (0, 0)), tokens, tokens],
-        out_specs=[tokens, block((D, step), lambda i: (0, i)), window],
+        in_specs=[SMEM, block((step, D), lambda i: (i, 0)), block((SLOT, D), lambda i: (0, 0)), tokens, tokens],
+        out_specs=[tokens, block((D, step), lambda i: (0, i)), block((COMMON, step), lambda i: (0, i))],
         scratch_shapes=[pltpu.VMEM((2, COMMON, SLOT), BF16)],
         compiler_params=params(28),
         cost_estimate=pl.CostEstimate(flops=2 * TOK * SLOT * (D + 2 * COMMON), bytes_accessed=16 << 20, transcendentals=0),
         name="hidden_grad",
-    )(where, alive, grad_out, weight[0], hidden, other)
+    )(plan, grad_out, weight[0], hidden, other)
     own = pl.pallas_call(
         merge_kernel,
         out_shape=shape((COMMON, TOK), BF16),
-        in_specs=[SMEM, SMEM, VMEM, VMEM],
+        in_specs=[SMEM, VMEM, VMEM, VMEM],
         out_specs=VMEM,
         compiler_params=params(24),
         name="merge",
-    )(where, alive, own, early)
+    )(plan, own, early, middle)
     payload = pl.pallas_call(
         partial_kernel,
         out_shape=shape((NEAR, FAR * ROWS + PAD, 128), I16),

time: 85.7 us -> 82.5 us (0.963)
  the two profiles are of different devices: /device:TPU:24 before, /device:TPU:1 now
where the time goes in v4:
time: 82.5 us; the launch traced here: 82.1 us
  blocking collectives  42.7 us (52%)
  Pallas kernels  14.6 us (18%)
  starting transfers between devices  11.5 us (14%)
  waiting for transfers between devices  6.95 us (8%)
  local copies, waits for them, and re-layouts  5.66 us (7%)
    all_to_all x2, blocking collectives, local(): lax.all_to_all(payload, 'rep', 0, 0, axis_index_groups=[[f * NEAR + n for...  42.7 us
    ppermute x1, starting transfers between devices, local(): other = lax.ppermute(hidden, 'tp', [(t, t ^ 1) for t in range(N_TP)])  8.79 us
    ppermute x1, waiting for transfers between devices, local(): lax.ppermute(late, 'tp', [(t, t + 2) for t in range(0, 14, 2)] + [(t, t -...  6.69 us
    pallas_call x1, Pallas kernels, local(): pl.pallas_call(hidden_kernel, grid=(TOK // step,), out_shape=[shape((TOK,...  5.84 us
    unnamed x12, local copies, waits for them, and re-layouts  5.66 us
    pallas_call x1, Pallas kernels, local(): pl.pallas_call(partial_kernel, out_shape=shape((NEAR, FAR * ROWS + PAD, 1...  2.56 us
    pallas_call x1, Pallas kernels, local(): pl.pallas_call(late_kernel, out_shape=[shape((COMMON, TOK), BF16), shape(...  2.14 us
  transfers between devices with their start and end apart: 4, of which 2 were waited for; matrix products, arithmetic and copies ran while one was open for 0% of the time, Pallas kernels for 13%

profile of v4, /device:TPU:1, one launch (start us, length us, event | category | flops | bytes accessed | tf_op | source)
XLA Modules:
  0.0 82.1 jit_solution(9647900559161680723)
XLA Ops:
  0.6 8.8 %collective-permute-start = (bf16[1024,512]{1,0:T(8,128)(2,1)}, bf16[1024,512]{1,0:T(8,128)(2,1)S(1)}, u32[]{:S(2)}, u32[]{:S(2)}) collective-permute-start(bf16[1024,512]{1,0:T(8,128)(2,1)} %hidden.1), channel_id=1, source_target_pairs={{0,1},{1,0},{2,3},{3,2},{4,5},{5,4},{6,7},{7,6},{8,9},{9,8},{10,11... | collective-permute-start | bytes 3145736 | tf_op jit(solution)/shard_map/ppermute | solution.py:200
  9.4 0.7 collective-permute-start.1
  10.2 1.5 %plan.1 = s32[16]{0:T(128)} custom-call(s32[16,32]{1,0:T(8,128)} %bitcast.5), custom_call_target="tpu_custom_call" | custom-call | tf_op jit(solution)/shard_map/plan/pallas_call | solution.py:202
  11.6 0.3 collective-permute-done.other
  11.9 0.0 copy-start
  11.9 1.2 %copy-done = bf16[1024,512]{1,0:T(8,128)(2,1)S(1)} copy-done((bf16[1024,512]{1,0:T(8,128)(2,1)S(1)}, bf16[1024,512]{1,0:T(8,128)(2,1)}, u32[]{:S(2)}) %copy-start) | copy-done | bytes 1048600
  13.1 0.0 copy-start.2
  13.1 0.7 copy-done.2
  13.8 0.0 copy-start.1
  13.8 0.0 copy-start.3
  13.8 2.1 %late_window.1 = (bf16[448,1024]{1,0:T(8,128)(2,1)S(1)}, bf16[64,1024]{1,0:T(8,128)(2,1)S(1)}) custom-call(s32[16]{0:T(128)S(1)} %copy-done.2, bf16[1024,512]{1,0:T(8,128)(2,1)S(1)} %copy-done, bf16[1024,512]{1,0:T(8,128)(2,1)S(1)} %collective-permute-done.other), custom_call_target="tpu_custom_call" | custom-call | tf_op jit(solution)/shard_map/late_window/pallas_call | solution.py:209
  15.9 1.3 %collective-permute-start.3 = (bf16[448,1024]{1,0:T(8,128)(2,1)S(1)}, bf16[448,1024]{1,0:T(8,128)(2,1)S(1)}, u32[]{:S(2)}, u32[]{:S(2)}) collective-permute-start(bf16[448,1024]{1,0:T(8,128)(2,1)S(1)} %get-tuple-element.11), channel_id=1, source_target_pairs={{0,2},{2,4},{4,6},{6,8},{8,10},{10,12},{12,14},{3,1},{5,3},{7,5},{... | collective-permute-start | bytes 2752520 | tf_op jit(solution)/shard_map/ppermute | solution.py:218
  17.2 0.7 collective-permute-start.2
  17.9 0.0 copy-done.1
  17.9 0.0 copy-done.3
  17.9 0.0 copy-start.4
  17.9 2.2 %copy-done.4 = bf16[1024,2048]{1,0:T(8,128)(2,1)S(1)} copy-done((bf16[1024,2048]{1,0:T(8,128)(2,1)S(1)}, bf16[1024,2048]{1,0:T(8,128)(2,1)}, u32[]{:S(2)}) %copy-start.4) | copy-done | bytes 4194328
  20.1 0.0 copy-start.5
  20.1 1.6 %copy-done.5 = bf16[1,512,2048]{2,1,0:T(8,128)(2,1)S(1)} copy-done((bf16[1,512,2048]{2,1,0:T(8,128)(2,1)S(1)}, bf16[1,512,2048]{2,1,0:T(8,128)(2,1)}, u32[]{:S(2)}) %copy-start.5) | copy-done | bytes 2097176
  21.7 5.8 %hidden_grad.1 = (bf16[1024,512]{1,0:T(8,128)(2,1)}, bf16[2048,1024]{1,0:T(8,128)(2,1)S(1)}, bf16[448,1024]{1,0:T(8,128)(2,1)S(1)}) custom-call(s32[16]{0:T(128)S(1)} %copy-done.3, bf16[1024,2048]{1,0:T(8,128)(2,1)S(1)} %copy-done.4, bf16[512,2048]{1,0:T(8,128)(2,1)S(1)} %bitcast.3, bf16[1024,512]{1,0:T(8,128)(2,1)S(1)} %copy-done.1, ...), custom_call_target="tpu_custom_call" | custom-call | flops 3087007744 | bytes 16777216 | tf_op jit(solution)/shard_map/hidden_grad/pallas_call | solution.py:222
  27.6 0.0 collective-permute-done.1.early
  27.6 0.0 collective-permute-done.2.middle
  27.6 1.2 %merge.1.local = bf16[448,1024]{1,0:T(8,128)(2,1)S(1)} custom-call(s32[16]{0:T(128)S(1)} %copy-done.3, bf16[448,1024]{1,0:T(8,128)(2,1)S(1)} %get-tuple-element.9.local, bf16[1024,512]{1,0:T(8,128)(2,1)S(1)} %collective-permute-done.1.early, bf16[64,1024]{1,0:T(8,128)(2,1)S(1)} %collective-permute-done.2.middle), custom_call_target="tpu_custom_call" | custom-call | tf_op jit(solution)/shard_map/merge/pallas_call | solution.py:233
  28.8 6.7 %collective-permute-done.3.late = bf16[448,1024]{1,0:T(8,128)(2,1)S(1)} collective-permute-done((bf16[448,1024]{1,0:T(8,128)(2,1)S(1)}, bf16[448,1024]{1,0:T(8,128)(2,1)S(1)}, u32[]{:S(2)}, u32[]{:S(2)}) %collective-permute-start.3) | collective-permute-done | bytes 917536 | tf_op jit(solution)/shard_map/ppermute | solution.py:218
  35.5 2.6 %partial.1 = s16[8,912,128]{2,1,0:T(8,128)(2,1)S(1)} custom-call(bf16[2048,1024]{1,0:T(8,128)(2,1)S(1)} %get-tuple-element.8.grad_t, bf16[448,1024]{1,0:T(8,128)(2,1)S(1)} %merge.1.local, bf16[448,1024]{1,0:T(8,128)(2,1)S(1)} %collective-permute-done.3.late), custom_call_target="tpu_custom_call" | custom-call | tf_op jit(solution)/shard_map/partial/pallas_call | solution.py:241
  38.1 25.3 %all_to_all.10.got = s16[8,912,128]{2,1,0:T(8,128)(2,1)S(1)} all-to-all(s16[8,912,128]{2,1,0:T(8,128)(2,1)S(1)} %partial.1), channel_id=1, replica_groups={{0,16,32,48,64,80,96,112},{128,144,160,176,192,208,224,240},{256,272,28..., dimensions={0} | all-to-all | bytes 3735552 | tf_op jit(solution)/shard_map/all_to_all | solution.py:250
  63.3 0.6 middle.1
  63.9 17.4 %all_to_all.11.got = s16[4,240,128]{2,1,0:T(8,128)(2,1)S(1)} all-to-all(s16[4,240,128]{2,1,0:T(8,128)(2,1)S(1)} %middle.1), channel_id=1, replica_groups={{0,128,256,384},{16,144,272,400},{32,160,288,416},{48,176,304,432},{64,..., dimensions={0} | all-to-all | bytes 491520 | tf_op jit(solution)/shard_map/all_to_all | solution.py:262
  81.3 0.8 final.1
Async XLA Ops:
  0.6 11.3 %collective-permute-start = (bf16[1024,512]{1,0:T(8,128)(2,1)}, bf16[1024,512]{1,0:T(8,128)(2,1)S(1)}, u32[]{:S(2)}, u32[]{:S(2)}) collective-permute-start(bf16[1024,512]{1,0:T(8,128)(2,1)} %hidden.1), channel_id=1, source_target_pairs={{0,1},{1,0},{2,3},{3,2},{4,5},{5,4},{6,7},{7,6},{8,9},{9,8},{10,11... | collective-permute-start | bytes 3145736 | tf_op jit(solution)/shard_map/ppermute | solution.py:200
  9.4 18.1 %collective-permute-start.1 = (bf16[1024,512]{1,0:T(8,128)(2,1)}, bf16[1024,512]{1,0:T(8,128)(2,1)S(1)}, u32[]{:S(2)}, u32[]{:S(2)}) collective-permute-start(bf16[1024,512]{1,0:T(8,128)(2,1)} %hidden.1), channel_id=1, source_target_pairs={{9,11},{11,13},{13,15},{2,0},{4,2},{6,4},{25,27},{27,29},{29,31},{... | collective-permute-start | bytes 3145736 | tf_op jit(solution)/shard_map/ppermute | solution.py:201
  11.9 1.2 %copy-start = (bf16[1024,512]{1,0:T(8,128)(2,1)S(1)}, bf16[1024,512]{1,0:T(8,128)(2,1)}, u32[]{:S(2)}) copy-start(bf16[1024,512]{1,0:T(8,128)(2,1)} %hidden.1) | copy-start | bytes 3145732
  13.1 0.7 copy-start.2
  13.8 4.1 %copy-start.1 = (bf16[1024,512]{1,0:T(8,128)(2,1)S(1)}, bf16[1024,512]{1,0:T(8,128)(2,1)}, u32[]{:S(2)}) copy-start(bf16[1024,512]{1,0:T(8,128)(2,1)} %hidden.1) | copy-start | bytes 3145732
  13.8 4.1 %copy-start.3 = (s32[16]{0:T(128)S(1)}, s32[16]{0:T(128)}, u32[]{:S(2)}) copy-start(s32[16]{0:T(128)} %plan.1) | copy-start | bytes 196
  15.9 19.6 %collective-permute-start.3 = (bf16[448,1024]{1,0:T(8,128)(2,1)S(1)}, bf16[448,1024]{1,0:T(8,128)(2,1)S(1)}, u32[]{:S(2)}, u32[]{:S(2)}) collective-permute-start(bf16[448,1024]{1,0:T(8,128)(2,1)S(1)} %get-tuple-element.11), channel_id=1, source_target_pairs={{0,2},{2,4},{4,6},{6,8},{8,10},{10,12},{12,14},{3,1},{5,3},{7,5},{... | collective-permute-start | bytes 2752520 | tf_op jit(solution)/shard_map/ppermute | solution.py:218
  17.2 10.3 %collective-permute-start.2 = (bf16[64,1024]{1,0:T(8,128)(2,1)S(1)}, bf16[64,1024]{1,0:T(8,128)(2,1)S(1)}, u32[]{:S(2)}, u32[]{:S(2)}) collective-permute-start(bf16[64,1024]{1,0:T(8,128)(2,1)S(1)} %get-tuple-element.10), channel_id=1, source_target_pairs={{7,9},{8,6},{23,25},{24,22},{39,41},{40,38},{55,57},{56,54},{71,73... | collective-permute-start | bytes 393224 | tf_op jit(solution)/shard_map/ppermute | solution.py:219
  17.9 2.2 %copy-start.4 = (bf16[1024,2048]{1,0:T(8,128)(2,1)S(1)}, bf16[1024,2048]{1,0:T(8,128)(2,1)}, u32[]{:S(2)}) copy-start(bf16[1024,2048]{1,0:T(8,128)(2,1)} %grad.1) | copy-start | bytes 12582916
  20.1 1.6 %copy-start.5 = (bf16[1,512,2048]{2,1,0:T(8,128)(2,1)S(1)}, bf16[1,512,2048]{2,1,0:T(8,128)(2,1)}, u32[]{:S(2)}) copy-start(bf16[1,512,2048]{2,1,0:T(8,128)(2,1)} %param.6) | copy-start | bytes 6291460

commit v5 on v4

v5 whole, which is shorter than its diff:
```python
import functools

import jax
import jax.numpy as jnp
from jax import lax
from jax.experimental import pallas as pl
from jax.experimental.pallas import tpu as pltpu
from jax.sharding import PartitionSpec as P

FF = 7168
TOK, D, SLOT, COMMON = 1024, 2048, 512, 448
N_REP, N_TP = 32, 16
NEAR, FAR = 8, 4
ROWS = 224
GROUPS = ((0, 64), (64, 64), (128, 64), (192, 32))
UNITS = ((0, 0, 128), (128, 256, 96), (224, 128, 128), (352, 352, 96))
PAD = 16
LOG_LEVELS = 14.999
MID = 64
WIDTH, LIMIT, LATE_OWN, LATE_OTHER, LOCAL_OWN, LOCAL_OTHER, EARLY, LIGHT, MIDDLE, ODD = range(10)
FACTOR = float(N_REP * TOK) ** -0.5
F32, BF16, I16 = jnp.float32, jnp.bfloat16, jnp.int16
VMEM = pl.BlockSpec(memory_space=pltpu.VMEM)
SMEM = pl.BlockSpec(memory_space=pltpu.SMEM)


def own_kernel(alive, own, plan, out, middle):
    replica, me = lax.axis_index("rep"), lax.axis_index("tp")
    live = jnp.int32(0)
    for t in range(N_TP):
        live += alive[t, replica]
    width = lax.div(jnp.int32(FF), live)

    def shift(device, slot):
        rank = jnp.int32(0)
        for t in range(N_TP):
            rank += jnp.where(t < device, alive[t, replica], 0)
        return jnp.where(alive[device, replica] == 1, slot * COMMON - rank * width, 4 * FF)

    other = me ^ 1
    back = even_odd(me, -2, 2)
    away = even_odd(me, 2, -2)
    plan[WIDTH] = width
    plan[LIMIT] = jnp.where(alive[me, replica] == 1, width, 0)
    plan[LATE_OWN] = shift(me, away)
    plan[LATE_OTHER] = shift(other, away)
    plan[LOCAL_OWN] = shift(me, me)
    plan[LOCAL_OTHER] = shift(other, me)
    plan[EARLY] = shift(jnp.clip(away, 0, N_TP - 1), me)
    plan[LIGHT] = shift(jnp.clip(even_odd(me, -1, 1), 0, N_TP - 1), me)
    plan[MIDDLE] = shift(me, back) + jnp.where(me % 2 == 0, COMMON - MID, 0)
    plan[ODD] = me % 2
    late = selection(width, plan[LATE_OWN])
    small = selection(width, plan[MIDDLE], MID)
    for i in range(0, TOK, 256):
        out[:, i : i + 256] = across(late, own[i : i + 256]).astype(BF16)
        middle[:, i : i + 256] = across(small, own[i : i + 256]).astype(BF16)


def selection(width, shift, wanted=COMMON):
    ahead = lax.broadcasted_iota(jnp.int32, (wanted, SLOT), 1) - lax.broadcasted_iota(jnp.int32, (wanted, SLOT), 0)
    cols = lax.broadcasted_iota(jnp.int32, (wanted, SLOT), 1)
    return ((ahead == shift) & (cols < width)).astype(F32).astype(BF16)


def across(a, b):
    return lax.dot_general(a, b, (((1,), (1,)), ((), ())), preferred_element_type=F32)


def even_odd(me, even, odd):
    return me + jnp.where(me % 2 == 0, even, odd)


def late_kernel(plan, own, other, out):
    late = selection(plan[WIDTH], plan[LATE_OTHER])
    for i in range(0, TOK, 256):
        out[:, i : i + 256] = own[:, i : i + 256] + across(late, other[i : i + 256]).astype(BF16)


def merge_kernel(plan, middle, light, early, local, out):
    width = plan[WIDTH]
    got = across(selection(width, plan[EARLY]), early[...])
    got += across(selection(width, plan[LIGHT]), light[...])
    out[...] = local[...] + got.astype(BF16)

    @pl.when(plan[ODD] == 1)
    def _():
        out[:MID] = out[:MID] + middle[...]

    @pl.when(plan[ODD] == 0)
    def _():
        out[COMMON - MID :] = out[COMMON - MID :] + middle[...]


def hidden_kernel(plan, grad, weight, own, other, grad_hidden, local, select):
    @pl.when(pl.program_id(0) == 0)
    def _():
        select[0] = selection(plan[WIDTH], plan[LOCAL_OWN])
        select[1] = selection(plan[WIDTH], plan[LOCAL_OTHER])

    block = grad[...]
    product = across(block, weight[...])
    cols = lax.broadcasted_iota(jnp.int32, product.shape, 1)
    grad_hidden[...] = jnp.where(cols < plan[LIMIT], product, 0.0).astype(BF16)
    local[...] = (across(select[0], own[...]) + across(select[1], other[...])).astype(BF16)


def steps_of(most):
    return jnp.ceil(256.0 * (jnp.log2(jnp.maximum(most, 1e-30)) - LOG_LEVELS))


def coded(value, inverse):
    return jnp.round(value * inverse).astype(jnp.int32).astype(I16)


def low_lanes(rows, below):
    return lax.broadcasted_iota(jnp.int32, (rows, 128), 1) < below


def fold(top, bottom):
    low = low_lanes(ROWS, 64)
    return jnp.where(low, top, pltpu.roll(bottom, 64, 1)), jnp.where(low, pltpu.roll(top, 64, 1), bottom)


def tallest(value):
    return jnp.max(jnp.abs(value).reshape(value.shape[0] // 8, 8, 128), axis=0)


def write_code(out, index, blocks, folded, most):
    steps = [steps_of(jnp.max(m, axis=0, keepdims=True)) for m in most]
    inverse = [jnp.exp2(step * (-1.0 / 256.0)) for step in steps]
    for block in range(blocks):
        for (row, rows), inv in zip(GROUPS, inverse):
            r = block * ROWS + row
            out[index, r : r + rows] = coded(folded(r, rows), inv)
    head = jnp.concatenate(steps + [jnp.zeros((PAD - len(steps), 128), F32)], axis=0)
    out[index, blocks * ROWS :] = head.astype(jnp.int32).astype(I16)


def read_steps(got, index, blocks):
    head = got[index, blocks * ROWS :].astype(jnp.int32).astype(F32)
    return jnp.exp2(head * (1.0 / 256.0))


def read_sum(got, sources, steps, r, rows, group):
    value = None
    for k in range(sources):
        term = got[k, r : r + rows].astype(jnp.int32).astype(F32) * steps[k][group : group + 1]
        value = term if value is None else value + term
    return value


def partial_kernel(grad, local, late, out, common, folded):
    for to, first, count in UNITS:
        common[to : to + count] = local[first : first + count] + late[first : first + count]
    wide = NEAR // 2 * 64
    for half in range(2):
        most = [[None] * len(GROUPS) for _ in range(NEAR)]
        for far in range(FAR):
            f = (far * 2 + half) * wide
            got = jnp.dot(common[...], grad[:, f : f + wide], preferred_element_type=F32)
            for c in range(0, wide, 128):
                near = half * (NEAR // 2) + c // 64
                for n, part in enumerate(fold(got[:ROWS, c : c + 128], got[ROWS:, c : c + 128]), near):
                    folded[n, far * ROWS : far * ROWS + ROWS] = part
                    for g, (row, rows) in enumerate(GROUPS):
                        big = tallest(part[row : row + rows])
                        most[n][g] = big if far == 0 else jnp.maximum(most[n][g], big)
        for n in range(half * (NEAR // 2), (half + 1) * (NEAR // 2)):
            write_code(out, n, FAR, lambda r, rows: folded[n, r : r + rows], most[n])


def middle_kernel(got, out, folded):
    steps = [read_steps(got, k, FAR) for k in range(NEAR)]
    for far in range(FAR):
        most = []
        for g, (row, rows) in enumerate(GROUPS):
            value = read_sum(got, NEAR, steps, far * ROWS + row, rows, g)
            folded[row : row + rows] = value
            most.append(tallest(value))
        write_code(out, far, 1, lambda r, rows: folded[r : r + rows], most)


def final_kernel(got, out, total):
    steps = [read_steps(got, k, 1) * FACTOR for k in range(FAR)]
    for g, (row, rows) in enumerate(GROUPS):
        total[row : row + rows] = read_sum(got, FAR, steps, row, rows, g)
    total[ROWS:] = jnp.zeros((256 - ROWS, 128), F32)
    turned = total[...].T
    out[:, :128] = turned[:64, :128]
    out[:, 128:256] = turned[64:, :128]
    rest = pltpu.roll(turned[64:, 128:], 96, 1)
    out[:, 256:384] = jnp.where(low_lanes(64, 96), turned[:64, 128:], rest)
    out[:, 384:] = rest[:, :64]


def shape(dims, kind):
    return jax.ShapeDtypeStruct(dims, kind)


def params(mib):
    return pltpu.CompilerParams(vmem_limit_bytes=mib << 20)


def block(dims, index):
    return pl.BlockSpec(dims, index)


def local(hidden, grad_out, weight, alive):
    early = lax.ppermute(hidden, "tp", [(t, t + 2) for t in (9, 11, 13)] + [(t, t - 2) for t in (2, 4, 6)])
    other = lax.ppermute(hidden, "tp", [(t, t ^ 1) for t in range(N_TP)])
    light = lax.ppermute(hidden, "tp", [(t, t - 1) for t in (10, 12, 14)] + [(t, t + 1) for t in (1, 3, 5)])
    plan, late, middle = pl.pallas_call(
        own_kernel,
        out_shape=[shape((16,), jnp.int32), shape((COMMON, TOK), BF16), shape((MID, TOK), BF16)],
        in_specs=[SMEM, VMEM],
        out_specs=[SMEM, VMEM, VMEM],
        compiler_params=params(24),
        name="own_window",
    )(alive.T, hidden)
    late = pl.pallas_call(
        late_kernel,
        out_shape=shape((COMMON, TOK), BF16),
        in_specs=[SMEM, VMEM, VMEM],
        out_specs=VMEM,
        compiler_params=params(24),
        name="late_window",
    )(plan, late, other)
    late = lax.ppermute(late, "tp", [(t, t + 2) for t in (6, 8, 10, 12)] + [(t, t - 2) for t in (3, 5, 7, 9)])
    middle = lax.ppermute(middle, "tp", [(7, 9), (8, 6)])
    step = 256
    tokens = block((step, SLOT), lambda i: (i, 0))
    grad_hidden, own = pl.pallas_call(
        hidden_kernel,
        grid=(TOK // step,),
        out_shape=[shape((TOK, SLOT), BF16), shape((COMMON, TOK), BF16)],
        in_specs=[SMEM, block((step, D), lambda i: (i, 0)), block((SLOT, D), lambda i: (0, 0)), tokens, tokens],
        out_specs=[tokens, block((COMMON, step), lambda i: (0, i))],
        scratch_shapes=[pltpu.VMEM((2, COMMON, SLOT), BF16)],
        compiler_params=params(50),
        cost_estimate=pl.CostEstimate(flops=2 * TOK * SLOT * (D + 2 * COMMON), bytes_accessed=16 << 20, transcendentals=0),
        name="hidden_grad",
    )(plan, grad_out, weight[0], hidden, other)
    own = pl.pallas_call(
        merge_kernel,
        out_shape=shape((COMMON, TOK), BF16),
        in_specs=[SMEM, VMEM, VMEM, VMEM, VMEM],
        out_specs=VMEM,
        compiler_params=params(24),
        name="merge",
    )(plan, middle, light, early, own)
    payload = pl.pallas_call(
        partial_kernel,
        out_shape=shape((NEAR, FAR * ROWS + PAD, 128), I16),
        in_specs=[VMEM] * 3,
        out_specs=VMEM,
        scratch_shapes=[pltpu.VMEM((COMMON, TOK), BF16), pltpu.VMEM((NEAR, FAR * ROWS, 128), F32)],
        compiler_params=params(32),
        name="partial",
    )(grad_out, own, late)
    payload = lax.all_to_all(
        payload, "rep", 0, 0, axis_index_groups=[[f * NEAR + n for n in range(NEAR)] for f in range(FAR)]
    )
    payload = pl.pallas_call(
        middle_kernel,
        out_shape=shape((FAR, ROWS + PAD, 128), I16),
        in_specs=[VMEM],
        out_specs=VMEM,
        scratch_shapes=[pltpu.VMEM((ROWS, 128), F32)],
        compiler_params=params(16),
        name="middle",
    )(payload)
    payload = lax.all_to_all(
        payload, "rep", 0, 0, axis_index_groups=[[f * NEAR + n for f in range(FAR)] for n in range(NEAR)]
    )
    grad_weight_t = pl.pallas_call(
        final_kernel,
        out_shape=shape((64, COMMON), F32),
        in_specs=[VMEM],
        out_specs=VMEM,
        scratch_shapes=[pltpu.VMEM((256, 128), F32)],
        compiler_params=params(16),
        name="final",
    )(payload)
    return grad_hidden, grad_weight_t.T


def solution(mesh):
    return jax.shard_map(
        local,
        mesh=mesh,
        in_specs=(P("rep", "tp"), P("rep", None), P("rep", "tp", None), P()),
        out_specs=(P("rep", "tp"), P("tp", "rep")),
        check_vma=False,
    )
```

time: 82.5 us -> 82 us (level)
  the two profiles are of different devices: /device:TPU:1 before, /device:TPU:24 now
where the time goes in v5:
time: 82 us; the launch traced here: 81.6 us
  blocking collectives  51.6 us (63%)
  Pallas kernels  15.7 us (19%)
  starting transfers between devices  9.41 us (11%)
  waiting for transfers between devices  2.27 us (3%)
  local copies, waits for them, and re-layouts  1.92 us (2%)
    all_to_all x2, blocking collectives, local(): lax.all_to_all(payload, 'rep', 0, 0, axis_index_groups=[[f * NEAR + n for...  51.6 us
    pallas_call x1, Pallas kernels, local(): pl.pallas_call(hidden_kernel, grid=(TOK // step,), out_shape=[shape((TOK,...  7.07 us
    pallas_call x1, Pallas kernels, local(): pl.pallas_call(partial_kernel, out_shape=shape((NEAR, FAR * ROWS + PAD, 1...  2.58 us
    ppermute x1, starting transfers between devices, local(): lax.ppermute(late, 'tp', [(t, t + 2) for t in (6, 8, 10, 12)] + [(t, t -...  2.49 us
    ppermute x1, starting transfers between devices, local(): lax.ppermute(hidden, 'tp', [(t, t + 2) for t in (9, 11, 13)] + [(t, t - 2...  2.42 us
    ppermute x1, waiting for transfers between devices, local(): middle = lax.ppermute(middle, 'tp', [(7, 9), (8, 6)])  2.26 us
    unnamed x8, local copies, waits for them, and re-layouts  1.92 us
    ppermute x1, starting transfers between devices, local(): other = lax.ppermute(hidden, 'tp', [(t, t ^ 1) for t in range(N_TP)])  1.92 us
  transfers between devices with their start and end apart: 5, of which 1 were waited for; matrix products, arithmetic and copies ran while one was open for 0% of the time, Pallas kernels for 14%

profile of v5, /device:TPU:24, one launch (start us, length us, event | category | flops | bytes accessed | tf_op | source)
XLA Modules:
  0.0 81.6 jit_solution(3025168630467362138)
XLA Ops:
  0.6 1.9 %collective-permute-start = (bf16[1024,512]{1,0:T(8,128)(2,1)}, bf16[1024,512]{1,0:T(8,128)(2,1)S(1)}, u32[]{:S(2)}, u32[]{:S(2)}) collective-permute-start(bf16[1024,512]{1,0:T(8,128)(2,1)} %own.3), channel_id=1, source_target_pairs={{0,1},{1,0},{2,3},{3,2},{4,5},{5,4},{6,7},{7,6},{8,9},{9,8},{10,11... | collective-permute-start | bytes 3145736 | tf_op jit(solution)/shard_map/ppermute | solution.py:211
  2.6 2.4 %collective-permute-start.3 = (bf16[1024,512]{1,0:T(8,128)(2,1)}, bf16[1024,512]{1,0:T(8,128)(2,1)S(1)}, u32[]{:S(2)}, u32[]{:S(2)}) collective-permute-start(bf16[1024,512]{1,0:T(8,128)(2,1)} %own.3), channel_id=1, source_target_pairs={{9,11},{11,13},{13,15},{2,0},{4,2},{6,4},{25,27},{27,29},{29,31},{... | collective-permute-start | bytes 3145736 | tf_op jit(solution)/shard_map/ppermute | solution.py:210
  5.0 1.3 %collective-permute-start.2 = (bf16[1024,512]{1,0:T(8,128)(2,1)}, bf16[1024,512]{1,0:T(8,128)(2,1)S(1)}, u32[]{:S(2)}, u32[]{:S(2)}) collective-permute-start(bf16[1024,512]{1,0:T(8,128)(2,1)} %own.3), channel_id=1, source_target_pairs={{10,9},{12,11},{14,13},{1,2},{3,4},{5,6},{26,25},{28,27},{30,29},{... | collective-permute-start | bytes 3145736 | tf_op jit(solution)/shard_map/ppermute | solution.py:212
  6.3 0.0 copy-start.1
  6.3 1.2 %copy-done.1 = bf16[1024,512]{1,0:T(8,128)(2,1)S(1)} copy-done((bf16[1024,512]{1,0:T(8,128)(2,1)S(1)}, bf16[1024,512]{1,0:T(8,128)(2,1)}, u32[]{:S(2)}) %copy-start.1) | copy-done | bytes 1048600
  7.5 0.0 copy-start.3
  7.5 0.7 copy-done.3
  8.2 0.0 copy-start.2
  8.2 1.7 %own_window.1 = (s32[16]{0:T(128)S(1)}, bf16[448,1024]{1,0:T(8,128)(2,1)S(1)}, bf16[64,1024]{1,0:T(8,128)(2,1)S(1)}) custom-call(s32[16,32]{1,0:T(8,128)S(1)} %bitcast.3, bf16[1024,512]{1,0:T(8,128)(2,1)S(1)} %copy-done.1), custom_call_target="tpu_custom_call" | custom-call | tf_op jit(solution)/shard_map/own_window/pallas_call | solution.py:213
  9.9 0.0 collective-permute-done.other
  9.9 1.2 %late_window.1 = bf16[448,1024]{1,0:T(8,128)(2,1)S(1)} custom-call(s32[16]{0:T(128)S(1)} %get-tuple-element.7.plan, bf16[448,1024]{1,0:T(8,128)(2,1)S(1)} %get-tuple-element.11.own, bf16[1024,512]{1,0:T(8,128)(2,1)S(1)} %collective-permute-done.other), custom_call_target="tpu_custom_call" | custom-call | tf_op jit(solution)/shard_map/late_window/pallas_call | solution.py:221
  11.1 2.5 %collective-permute-start.4 = (bf16[448,1024]{1,0:T(8,128)(2,1)S(1)}, bf16[448,1024]{1,0:T(8,128)(2,1)S(1)}, u32[]{:S(2)}, u32[]{:S(2)}) collective-permute-start(bf16[448,1024]{1,0:T(8,128)(2,1)S(1)} %late_window.1), channel_id=1, source_target_pairs={{6,8},{8,10},{10,12},{12,14},{3,1},{5,3},{7,5},{9,7},{22,24},{24,2... | collective-permute-start | bytes 2752520 | tf_op jit(solution)/shard_map/ppermute | solution.py:229
  13.6 1.3 %collective-permute-start.1 = (bf16[64,1024]{1,0:T(8,128)(2,1)S(1)}, bf16[64,1024]{1,0:T(8,128)(2,1)S(1)}, u32[]{:S(2)}, u32[]{:S(2)}) collective-permute-start(bf16[64,1024]{1,0:T(8,128)(2,1)S(1)} %get-tuple-element.9), channel_id=1, source_target_pairs={{7,9},{8,6},{23,25},{24,22},{39,41},{40,38},{55,57},{56,54},{71,73... | collective-permute-start | bytes 393224 | tf_op jit(solution)/shard_map/ppermute | solution.py:230
  14.9 0.0 copy-done.2
  14.9 0.0 copy-start
  14.9 7.1 %hidden_grad.1 = (bf16[1024,512]{1,0:T(8,128)(2,1)}, bf16[448,1024]{1,0:T(8,128)(2,1)S(1)}) custom-call(s32[16]{0:T(128)S(1)} %get-tuple-element.7.plan, bf16[1024,2048]{1,0:T(8,128)(2,1)} %grad.3, bf16[512,2048]{1,0:T(8,128)(2,1)} %bitcast.5, bf16[1024,512]{1,0:T(8,128)(2,1)S(1)} %copy-done.2, bf16[1024,512]{1,0:T(8,128)(2,1)S(1)} %collective-permute-done.other), custom_call_target="tpu_custom_call" | custom-call | flops 3087007744 | bytes 16777216 | tf_op jit(solution)/shard_map/hidden_grad/pallas_call | solution.py:233
  22.0 2.3 %collective-permute-done.1.middle = bf16[64,1024]{1,0:T(8,128)(2,1)S(1)} collective-permute-done((bf16[64,1024]{1,0:T(8,128)(2,1)S(1)}, bf16[64,1024]{1,0:T(8,128)(2,1)S(1)}, u32[]{:S(2)}, u32[]{:S(2)}) %collective-permute-start.1) | collective-permute-done | bytes 131104 | tf_op jit(solution)/shard_map/ppermute | solution.py:230
  24.3 0.0 collective-permute-done.3.early
  24.3 0.0 collective-permute-done.2.light
  24.3 1.7 %merge.1.local = bf16[448,1024]{1,0:T(8,128)(2,1)S(1)} custom-call(s32[16]{0:T(128)S(1)} %get-tuple-element.7.plan, bf16[64,1024]{1,0:T(8,128)(2,1)S(1)} %collective-permute-done.1.middle, bf16[1024,512]{1,0:T(8,128)(2,1)S(1)} %collective-permute-done.2.light, bf16[1024,512]{1,0:T(8,128)(2,1)S(1)} %collective-permute-done.3.early, ...), custom_call_target="tpu_custom_call" | custom-call | tf_op jit(solution)/shard_map/merge/pallas_call | solution.py:244
  26.0 0.0 collective-permute-done.4.late
  26.0 0.0 copy-done
  26.0 2.6 %partial.1 = s16[8,912,128]{2,1,0:T(8,128)(2,1)S(1)} custom-call(bf16[1024,2048]{1,0:T(8,128)(2,1)S(1)} %copy-done, bf16[448,1024]{1,0:T(8,128)(2,1)S(1)} %merge.1.local, bf16[448,1024]{1,0:T(8,128)(2,1)S(1)} %collective-permute-done.4.late), custom_call_target="tpu_custom_call" | custom-call | tf_op jit(solution)/shard_map/partial/pallas_call | solution.py:252
  28.6 31.6 %all_to_all.10.got = s16[8,912,128]{2,1,0:T(8,128)(2,1)S(1)} all-to-all(s16[8,912,128]{2,1,0:T(8,128)(2,1)S(1)} %partial.1), channel_id=1, replica_groups={{0,16,32,48,64,80,96,112},{128,144,160,176,192,208,224,240},{256,272,28..., dimensions={0} | all-to-all | bytes 3735552 | tf_op jit(solution)/shard_map/all_to_all | solution.py:261
  60.3 0.6 middle.1
  60.8 19.9 %all_to_all.11.got = s16[4,240,128]{2,1,0:T(8,128)(2,1)S(1)} all-to-all(s16[4,240,128]{2,1,0:T(8,128)(2,1)S(1)} %middle.1), channel_id=1, replica_groups={{0,128,256,384},{16,144,272,400},{32,160,288,416},{48,176,304,432},{64,..., dimensions={0} | all-to-all | bytes 491520 | tf_op jit(solution)/shard_map/all_to_all | solution.py:273
  80.8 0.8 %final.1 = f32[64,448]{1,0:T(8,128)} custom-call(s16[4,240,128]{2,1,0:T(8,128)(2,1)S(1)} %all_to_all.11.got), custom_call_target="tpu_custom_call" | custom-call | tf_op jit(solution)/shard_map/final/pallas_call | solution.py:276
Async XLA Ops:
  0.6 9.3 %collective-permute-start = (bf16[1024,512]{1,0:T(8,128)(2,1)}, bf16[1024,512]{1,0:T(8,128)(2,1)S(1)}, u32[]{:S(2)}, u32[]{:S(2)}) collective-permute-start(bf16[1024,512]{1,0:T(8,128)(2,1)} %own.3), channel_id=1, source_target_pairs={{0,1},{1,0},{2,3},{3,2},{4,5},{5,4},{6,7},{7,6},{8,9},{9,8},{10,11... | collective-permute-start | bytes 3145736 | tf_op jit(solution)/shard_map/ppermute | solution.py:211
  2.6 21.7 %collective-permute-start.3 = (bf16[1024,512]{1,0:T(8,128)(2,1)}, bf16[1024,512]{1,0:T(8,128)(2,1)S(1)}, u32[]{:S(2)}, u32[]{:S(2)}) collective-permute-start(bf16[1024,512]{1,0:T(8,128)(2,1)} %own.3), channel_id=1, source_target_pairs={{9,11},{11,13},{13,15},{2,0},{4,2},{6,4},{25,27},{27,29},{29,31},{... | collective-permute-start | bytes 3145736 | tf_op jit(solution)/shard_map/ppermute | solution.py:210
  5.0 19.3 %collective-permute-start.2 = (bf16[1024,512]{1,0:T(8,128)(2,1)}, bf16[1024,512]{1,0:T(8,128)(2,1)S(1)}, u32[]{:S(2)}, u32[]{:S(2)}) collective-permute-start(bf16[1024,512]{1,0:T(8,128)(2,1)} %own.3), channel_id=1, source_target_pairs={{10,9},{12,11},{14,13},{1,2},{3,4},{5,6},{26,25},{28,27},{30,29},{... | collective-permute-start | bytes 3145736 | tf_op jit(solution)/shard_map/ppermute | solution.py:212
  6.3 1.2 %copy-start.1 = (bf16[1024,512]{1,0:T(8,128)(2,1)S(1)}, bf16[1024,512]{1,0:T(8,128)(2,1)}, u32[]{:S(2)}) copy-start(bf16[1024,512]{1,0:T(8,128)(2,1)} %own.3) | copy-start | bytes 3145732
  7.5 0.7 copy-start.3
  8.2 6.7 %copy-start.2 = (bf16[1024,512]{1,0:T(8,128)(2,1)S(1)}, bf16[1024,512]{1,0:T(8,128)(2,1)}, u32[]{:S(2)}) copy-start(bf16[1024,512]{1,0:T(8,128)(2,1)} %own.3) | copy-start | bytes 3145732
  11.1 14.9 %collective-permute-start.4 = (bf16[448,1024]{1,0:T(8,128)(2,1)S(1)}, bf16[448,1024]{1,0:T(8,128)(2,1)S(1)}, u32[]{:S(2)}, u32[]{:S(2)}) collective-permute-start(bf16[448,1024]{1,0:T(8,128)(2,1)S(1)} %late_window.1), channel_id=1, source_target_pairs={{6,8},{8,10},{10,12},{12,14},{3,1},{5,3},{7,5},{9,7},{22,24},{24,2... | collective-permute-start | bytes 2752520 | tf_op jit(solution)/shard_map/ppermute | solution.py:229
  13.6 10.6 %collective-permute-start.1 = (bf16[64,1024]{1,0:T(8,128)(2,1)S(1)}, bf16[64,1024]{1,0:T(8,128)(2,1)S(1)}, u32[]{:S(2)}, u32[]{:S(2)}) collective-permute-start(bf16[64,1024]{1,0:T(8,128)(2,1)S(1)} %get-tuple-element.9), channel_id=1, source_target_pairs={{7,9},{8,6},{23,25},{24,22},{39,41},{40,38},{55,57},{56,54},{71,73... | collective-permute-start | bytes 393224 | tf_op jit(solution)/shard_map/ppermute | solution.py:230
  14.9 11.1 %copy-start = (bf16[1024,2048]{1,0:T(8,128)(2,1)S(1)}, bf16[1024,2048]{1,0:T(8,128)(2,1)}, u32[]{:S(2)}) copy-start(bf16[1024,2048]{1,0:T(8,128)(2,1)} %grad.3) | copy-start | bytes 12582916

commit v6 on v5

--- a/solution.py
+++ b/solution.py
@@ -17,7 +17,7 @@
 PAD = 16
 LOG_LEVELS = 14.999
 MID = 64
-WIDTH, LIMIT, LATE_OWN, LATE_OTHER, LOCAL_OWN, LOCAL_OTHER, EARLY, LIGHT, MIDDLE, ODD = range(10)
+WIDTH, LIMIT, LATE_OWN, LATE_OTHER, LOCAL_OWN, LOCAL_OTHER, EARLY, LIGHT, MIDDLE, ODD, HAS_EARLY, HAS_LIGHT = range(12)
 FACTOR = float(N_REP * TOK) ** -0.5
 F32, BF16, I16 = jnp.float32, jnp.bfloat16, jnp.int16
 VMEM = pl.BlockSpec(memory_space=pltpu.VMEM)
@@ -50,6 +50,9 @@
     plan[LIGHT] = shift(jnp.clip(even_odd(me, -1, 1), 0, N_TP - 1), me)
     plan[MIDDLE] = shift(me, back) + jnp.where(me % 2 == 0, COMMON - MID, 0)
     plan[ODD] = me % 2
+    outer = jnp.where(me % 2 == 1, me, N_TP - 1 - me)
+    plan[HAS_EARLY] = jnp.where(outer >= 11, 1, 0)
+    plan[HAS_LIGHT] = jnp.where((outer >= 9) & (outer <= 13), 1, 0)
     late = selection(width, plan[LATE_OWN])
     small = selection(width, plan[MIDDLE], MID)
     for i in range(0, TOK, 256):
@@ -78,10 +81,12 @@
 
 
 def merge_kernel(plan, middle, light, early, local, out):
-    width = plan[WIDTH]
-    got = across(selection(width, plan[EARLY]), early[...])
-    got += across(selection(width, plan[LIGHT]), light[...])
-    out[...] = local[...] + got.astype(BF16)
+    out[...] = local[...]
+    for flag, shift, block in ((HAS_EARLY, EARLY, early), (HAS_LIGHT, LIGHT, light)):
+
+        @pl.when(plan[flag] == 1)
+        def _():
+            out[...] = out[...] + across(selection(plan[WIDTH], plan[shift]), block[...]).astype(BF16)
 
     @pl.when(plan[ODD] == 1)
     def _():

time: 82 us -> 81.8 us (level)
  transfers between devices with their start and end apart: 5 -> 5, of which waited for: 1 -> 2; matrix products, arithmetic and copies ran while one was open for 0% -> 0% of each run, Pallas kernels for 14% -> 14%
where the time goes in v6:
time: 81.8 us; the launch traced here: 81.4 us
  blocking collectives  51.5 us (63%)
  Pallas kernels  15.3 us (19%)
  starting transfers between devices  9.41 us (12%)
  waiting for transfers between devices  2.54 us (3%)
  local copies, waits for them, and re-layouts  1.92 us (2%)
    all_to_all x2, blocking collectives, local(): lax.all_to_all(payload, 'rep', 0, 0, axis_index_groups=[[f * NEAR + n for...  51.5 us
    pallas_call x1, Pallas kernels, local(): pl.pallas_call(hidden_kernel, grid=(TOK // step,), out_shape=[shape((TOK,...  7.07 us
    pallas_call x1, Pallas kernels, local(): pl.pallas_call(partial_kernel, out_shape=shape((NEAR, FAR * ROWS + PAD, 1...  2.58 us
    ppermute x1, starting transfers between devices, local(): lax.ppermute(late, 'tp', [(t, t + 2) for t in (6, 8, 10, 12)] + [(t, t -...  2.49 us
    ppermute x1, starting transfers between devices, local(): lax.ppermute(hidden, 'tp', [(t, t + 2) for t in (9, 11, 13)] + [(t, t - 2...  2.42 us
    ppermute x1, waiting for transfers between devices, local(): middle = lax.ppermute(middle, 'tp', [(7, 9), (8, 6)])  2.26 us
    unnamed x8, local copies, waits for them, and re-layouts  1.92 us
    ppermute x1, starting transfers between devices, local(): other = lax.ppermute(hidden, 'tp', [(t, t ^ 1) for t in range(N_TP)])  1.92 us
  transfers between devices with their start and end apart: 5, of which 2 were waited for; matrix products, arithmetic and copies ran while one was open for 0% of the time, Pallas kernels for 14%

profile of v6, /device:TPU:24, one launch (start us, length us, event | category | flops | bytes accessed | tf_op | source)
XLA Modules:
  0.0 81.4 jit_solution(13173528007550354517)
XLA Ops:
  0.6 1.9 %collective-permute-start = (bf16[1024,512]{1,0:T(8,128)(2,1)}, bf16[1024,512]{1,0:T(8,128)(2,1)S(1)}, u32[]{:S(2)}, u32[]{:S(2)}) collective-permute-start(bf16[1024,512]{1,0:T(8,128)(2,1)} %own.3), channel_id=1, source_target_pairs={{0,1},{1,0},{2,3},{3,2},{4,5},{5,4},{6,7},{7,6},{8,9},{9,8},{10,11... | collective-permute-start | bytes 3145736 | tf_op jit(solution)/shard_map/ppermute | solution.py:216
  2.6 2.4 %collective-permute-start.3 = (bf16[1024,512]{1,0:T(8,128)(2,1)}, bf16[1024,512]{1,0:T(8,128)(2,1)S(1)}, u32[]{:S(2)}, u32[]{:S(2)}) collective-permute-start(bf16[1024,512]{1,0:T(8,128)(2,1)} %own.3), channel_id=1, source_target_pairs={{9,11},{11,13},{13,15},{2,0},{4,2},{6,4},{25,27},{27,29},{29,31},{... | collective-permute-start | bytes 3145736 | tf_op jit(solution)/shard_map/ppermute | solution.py:215
  5.0 1.3 %collective-permute-start.2 = (bf16[1024,512]{1,0:T(8,128)(2,1)}, bf16[1024,512]{1,0:T(8,128)(2,1)S(1)}, u32[]{:S(2)}, u32[]{:S(2)}) collective-permute-start(bf16[1024,512]{1,0:T(8,128)(2,1)} %own.3), channel_id=1, source_target_pairs={{10,9},{12,11},{14,13},{1,2},{3,4},{5,6},{26,25},{28,27},{30,29},{... | collective-permute-start | bytes 3145736 | tf_op jit(solution)/shard_map/ppermute | solution.py:217
  6.3 0.0 copy-start.1
  6.3 1.2 %copy-done.1 = bf16[1024,512]{1,0:T(8,128)(2,1)S(1)} copy-done((bf16[1024,512]{1,0:T(8,128)(2,1)S(1)}, bf16[1024,512]{1,0:T(8,128)(2,1)}, u32[]{:S(2)}) %copy-start.1) | copy-done | bytes 1048600
  7.5 0.0 copy-start.3
  7.5 0.7 copy-done.3
  8.2 0.0 copy-start.2
  8.2 1.7 %own_window.1 = (s32[16]{0:T(128)S(1)}, bf16[448,1024]{1,0:T(8,128)(2,1)S(1)}, bf16[64,1024]{1,0:T(8,128)(2,1)S(1)}) custom-call(s32[16,32]{1,0:T(8,128)S(1)} %bitcast.3, bf16[1024,512]{1,0:T(8,128)(2,1)S(1)} %copy-done.1), custom_call_target="tpu_custom_call" | custom-call | tf_op jit(solution)/shard_map/own_window/pallas_call | solution.py:218
  9.9 0.0 collective-permute-done.other
  9.9 1.2 %late_window.1 = bf16[448,1024]{1,0:T(8,128)(2,1)S(1)} custom-call(s32[16]{0:T(128)S(1)} %get-tuple-element.7.plan, bf16[448,1024]{1,0:T(8,128)(2,1)S(1)} %get-tuple-element.11.own, bf16[1024,512]{1,0:T(8,128)(2,1)S(1)} %collective-permute-done.other), custom_call_target="tpu_custom_call" | custom-call | tf_op jit(solution)/shard_map/late_window/pallas_call | solution.py:226
  11.1 2.5 %collective-permute-start.4 = (bf16[448,1024]{1,0:T(8,128)(2,1)S(1)}, bf16[448,1024]{1,0:T(8,128)(2,1)S(1)}, u32[]{:S(2)}, u32[]{:S(2)}) collective-permute-start(bf16[448,1024]{1,0:T(8,128)(2,1)S(1)} %late_window.1), channel_id=1, source_target_pairs={{6,8},{8,10},{10,12},{12,14},{3,1},{5,3},{7,5},{9,7},{22,24},{24,2... | collective-permute-start | bytes 2752520 | tf_op jit(solution)/shard_map/ppermute | solution.py:234
  13.6 1.3 %collective-permute-start.1 = (bf16[64,1024]{1,0:T(8,128)(2,1)S(1)}, bf16[64,1024]{1,0:T(8,128)(2,1)S(1)}, u32[]{:S(2)}, u32[]{:S(2)}) collective-permute-start(bf16[64,1024]{1,0:T(8,128)(2,1)S(1)} %get-tuple-element.9), channel_id=1, source_target_pairs={{7,9},{8,6},{23,25},{24,22},{39,41},{40,38},{55,57},{56,54},{71,73... | collective-permute-start | bytes 393224 | tf_op jit(solution)/shard_map/ppermute | solution.py:235
  14.9 0.0 copy-done.2
  14.9 0.0 copy-start
  14.9 7.1 %hidden_grad.1 = (bf16[1024,512]{1,0:T(8,128)(2,1)}, bf16[448,1024]{1,0:T(8,128)(2,1)S(1)}) custom-call(s32[16]{0:T(128)S(1)} %get-tuple-element.7.plan, bf16[1024,2048]{1,0:T(8,128)(2,1)} %grad.3, bf16[512,2048]{1,0:T(8,128)(2,1)} %bitcast.5, bf16[1024,512]{1,0:T(8,128)(2,1)S(1)} %copy-done.2, bf16[1024,512]{1,0:T(8,128)(2,1)S(1)} %collective-permute-done.other), custom_call_target="tpu_custom_call" | custom-call | flops 3087007744 | bytes 16777216 | tf_op jit(solution)/shard_map/hidden_grad/pallas_call | solution.py:238
  22.0 2.3 %collective-permute-done.1.middle = bf16[64,1024]{1,0:T(8,128)(2,1)S(1)} collective-permute-done((bf16[64,1024]{1,0:T(8,128)(2,1)S(1)}, bf16[64,1024]{1,0:T(8,128)(2,1)S(1)}, u32[]{:S(2)}, u32[]{:S(2)}) %collective-permute-start.1) | collective-permute-done | bytes 131104 | tf_op jit(solution)/shard_map/ppermute | solution.py:235
  24.3 0.0 collective-permute-done.3.early
  24.3 0.0 collective-permute-done.2.light
  24.3 1.3 %merge.1.local = bf16[448,1024]{1,0:T(8,128)(2,1)S(1)} custom-call(s32[16]{0:T(128)S(1)} %get-tuple-element.7.plan, bf16[64,1024]{1,0:T(8,128)(2,1)S(1)} %collective-permute-done.1.middle, bf16[1024,512]{1,0:T(8,128)(2,1)S(1)} %collective-permute-done.2.light, bf16[1024,512]{1,0:T(8,128)(2,1)S(1)} %collective-permute-done.3.early, ...), custom_call_target="tpu_custom_call" | custom-call | tf_op jit(solution)/shard_map/merge/pallas_call | solution.py:249
  25.6 0.3 collective-permute-done.4.late
  25.9 0.0 copy-done
  25.9 2.6 %partial.1 = s16[8,912,128]{2,1,0:T(8,128)(2,1)S(1)} custom-call(bf16[1024,2048]{1,0:T(8,128)(2,1)S(1)} %copy-done, bf16[448,1024]{1,0:T(8,128)(2,1)S(1)} %merge.1.local, bf16[448,1024]{1,0:T(8,128)(2,1)S(1)} %collective-permute-done.4.late), custom_call_target="tpu_custom_call" | custom-call | tf_op jit(solution)/shard_map/partial/pallas_call | solution.py:257
  28.5 31.6 %all_to_all.10.got = s16[8,912,128]{2,1,0:T(8,128)(2,1)S(1)} all-to-all(s16[8,912,128]{2,1,0:T(8,128)(2,1)S(1)} %partial.1), channel_id=1, replica_groups={{0,16,32,48,64,80,96,112},{128,144,160,176,192,208,224,240},{256,272,28..., dimensions={0} | all-to-all | bytes 3735552 | tf_op jit(solution)/shard_map/all_to_all | solution.py:266
  60.0 0.6 middle.1
  60.6 20.0 %all_to_all.11.got = s16[4,240,128]{2,1,0:T(8,128)(2,1)S(1)} all-to-all(s16[4,240,128]{2,1,0:T(8,128)(2,1)S(1)} %middle.1), channel_id=1, replica_groups={{0,128,256,384},{16,144,272,400},{32,160,288,416},{48,176,304,432},{64,..., dimensions={0} | all-to-all | bytes 491520 | tf_op jit(solution)/shard_map/all_to_all | solution.py:278
  80.6 0.8 %final.1 = f32[64,448]{1,0:T(8,128)} custom-call(s16[4,240,128]{2,1,0:T(8,128)(2,1)S(1)} %all_to_all.11.got), custom_call_target="tpu_custom_call" | custom-call | tf_op jit(solution)/shard_map/final/pallas_call | solution.py:281
Async XLA Ops:
  0.6 9.3 %collective-permute-start = (bf16[1024,512]{1,0:T(8,128)(2,1)}, bf16[1024,512]{1,0:T(8,128)(2,1)S(1)}, u32[]{:S(2)}, u32[]{:S(2)}) collective-permute-start(bf16[1024,512]{1,0:T(8,128)(2,1)} %own.3), channel_id=1, source_target_pairs={{0,1},{1,0},{2,3},{3,2},{4,5},{5,4},{6,7},{7,6},{8,9},{9,8},{10,11... | collective-permute-start | bytes 3145736 | tf_op jit(solution)/shard_map/ppermute | solution.py:216
  2.6 21.7 %collective-permute-start.3 = (bf16[1024,512]{1,0:T(8,128)(2,1)}, bf16[1024,512]{1,0:T(8,128)(2,1)S(1)}, u32[]{:S(2)}, u32[]{:S(2)}) collective-permute-start(bf16[1024,512]{1,0:T(8,128)(2,1)} %own.3), channel_id=1, source_target_pairs={{9,11},{11,13},{13,15},{2,0},{4,2},{6,4},{25,27},{27,29},{29,31},{... | collective-permute-start | bytes 3145736 | tf_op jit(solution)/shard_map/ppermute | solution.py:215
  5.0 19.3 %collective-permute-start.2 = (bf16[1024,512]{1,0:T(8,128)(2,1)}, bf16[1024,512]{1,0:T(8,128)(2,1)S(1)}, u32[]{:S(2)}, u32[]{:S(2)}) collective-permute-start(bf16[1024,512]{1,0:T(8,128)(2,1)} %own.3), channel_id=1, source_target_pairs={{10,9},{12,11},{14,13},{1,2},{3,4},{5,6},{26,25},{28,27},{30,29},{... | collective-permute-start | bytes 3145736 | tf_op jit(solution)/shard_map/ppermute | solution.py:217
  6.3 1.2 %copy-start.1 = (bf16[1024,512]{1,0:T(8,128)(2,1)S(1)}, bf16[1024,512]{1,0:T(8,128)(2,1)}, u32[]{:S(2)}) copy-start(bf16[1024,512]{1,0:T(8,128)(2,1)} %own.3) | copy-start | bytes 3145732
  7.5 0.7 copy-start.3
  8.2 6.7 %copy-start.2 = (bf16[1024,512]{1,0:T(8,128)(2,1)S(1)}, bf16[1024,512]{1,0:T(8,128)(2,1)}, u32[]{:S(2)}) copy-start(bf16[1024,512]{1,0:T(8,128)(2,1)} %own.3) | copy-start | bytes 3145732
  11.1 14.7 %collective-permute-start.4 = (bf16[448,1024]{1,0:T(8,128)(2,1)S(1)}, bf16[448,1024]{1,0:T(8,128)(2,1)S(1)}, u32[]{:S(2)}, u32[]{:S(2)}) collective-permute-start(bf16[448,1024]{1,0:T(8,128)(2,1)S(1)} %late_window.1), channel_id=1, source_target_pairs={{6,8},{8,10},{10,12},{12,14},{3,1},{5,3},{7,5},{9,7},{22,24},{24,2... | collective-permute-start | bytes 2752520 | tf_op jit(solution)/shard_map/ppermute | solution.py:234
  13.6 10.6 %collective-permute-start.1 = (bf16[64,1024]{1,0:T(8,128)(2,1)S(1)}, bf16[64,1024]{1,0:T(8,128)(2,1)S(1)}, u32[]{:S(2)}, u32[]{:S(2)}) collective-permute-start(bf16[64,1024]{1,0:T(8,128)(2,1)S(1)} %get-tuple-element.9), channel_id=1, source_target_pairs={{7,9},{8,6},{23,25},{24,22},{39,41},{40,38},{55,57},{56,54},{71,73... | collective-permute-start | bytes 393224 | tf_op jit(solution)/shard_map/ppermute | solution.py:235
  14.9 10.9 %copy-start = (bf16[1024,2048]{1,0:T(8,128)(2,1)S(1)}, bf16[1024,2048]{1,0:T(8,128)(2,1)}, u32[]{:S(2)}) copy-start(bf16[1024,2048]{1,0:T(8,128)(2,1)} %grad.3) | copy-start | bytes 12582916

commit v7 on v6

--- a/solution.py
+++ b/solution.py
@@ -55,9 +55,9 @@
     plan[HAS_LIGHT] = jnp.where((outer >= 9) & (outer <= 13), 1, 0)
     late = selection(width, plan[LATE_OWN])
     small = selection(width, plan[MIDDLE], MID)
-    for i in range(0, TOK, 256):
-        out[:, i : i + 256] = across(late, own[i : i + 256]).astype(BF16)
-        middle[:, i : i + 256] = across(small, own[i : i + 256]).astype(BF16)
+    for i in range(0, TOK, 512):
+        out[:, i : i + 512] = across(late, own[i : i + 512]).astype(BF16)
+        middle[:, i : i + 512] = across(small, own[i : i + 512]).astype(BF16)
 
 
 def selection(width, shift, wanted=COMMON):
@@ -76,8 +76,8 @@
 
 def late_kernel(plan, own, other, out):
     late = selection(plan[WIDTH], plan[LATE_OTHER])
-    for i in range(0, TOK, 256):
-        out[:, i : i + 256] = own[:, i : i + 256] + across(late, other[i : i + 256]).astype(BF16)
+    for i in range(0, TOK, 512):
+        out[:, i : i + 512] = own[:, i : i + 512] + across(late, other[i : i + 512]).astype(BF16)
 
 
 def merge_kernel(plan, middle, light, early, local, out):

time: 81.8 us -> 81.8 us (level)
  no operation moved by 1% of the time
where the time goes in v7:
time: 81.8 us; the launch traced here: 81.4 us
  blocking collectives  51.5 us (63%)
  Pallas kernels  15.2 us (19%)
  starting transfers between devices  9.43 us (12%)
  waiting for transfers between devices  2.53 us (3%)
  local copies, waits for them, and re-layouts  1.92 us (2%)
    all_to_all x2, blocking collectives, local(): lax.all_to_all(payload, 'rep', 0, 0, axis_index_groups=[[f * NEAR + n for...  51.5 us
    pallas_call x1, Pallas kernels, local(): pl.pallas_call(hidden_kernel, grid=(TOK // step,), out_shape=[shape((TOK,...  7.07 us
    pallas_call x1, Pallas kernels, local(): pl.pallas_call(partial_kernel, out_shape=shape((NEAR, FAR * ROWS + PAD, 1...  2.58 us
    ppermute x1, starting transfers between devices, local(): lax.ppermute(late, 'tp', [(t, t + 2) for t in (6, 8, 10, 12)] + [(t, t -...  2.5 us
    ppermute x1, starting transfers between devices, local(): lax.ppermute(hidden, 'tp', [(t, t + 2) for t in (9, 11, 13)] + [(t, t - 2...  2.42 us
    ppermute x1, waiting for transfers between devices, local(): middle = lax.ppermute(middle, 'tp', [(7, 9), (8, 6)])  2.25 us
    unnamed x8, local copies, waits for them, and re-layouts  1.92 us
    ppermute x1, starting transfers between devices, local(): other = lax.ppermute(hidden, 'tp', [(t, t ^ 1) for t in range(N_TP)])  1.92 us
  transfers between devices with their start and end apart: 5, of which 2 were waited for; matrix products, arithmetic and copies ran while one was open for 0% of the time, Pallas kernels for 14%

profile of v7, /device:TPU:24, one launch (start us, length us, event | category | flops | bytes accessed | tf_op | source)
XLA Modules:
  0.0 81.4 jit_solution(6741599876304134144)
XLA Ops:
  0.6 1.9 %collective-permute-start = (bf16[1024,512]{1,0:T(8,128)(2,1)}, bf16[1024,512]{1,0:T(8,128)(2,1)S(1)}, u32[]{:S(2)}, u32[]{:S(2)}) collective-permute-start(bf16[1024,512]{1,0:T(8,128)(2,1)} %own.3), channel_id=1, source_target_pairs={{0,1},{1,0},{2,3},{3,2},{4,5},{5,4},{6,7},{7,6},{8,9},{9,8},{10,11... | collective-permute-start | bytes 3145736 | tf_op jit(solution)/shard_map/ppermute | solution.py:216
  2.6 2.4 %collective-permute-start.3 = (bf16[1024,512]{1,0:T(8,128)(2,1)}, bf16[1024,512]{1,0:T(8,128)(2,1)S(1)}, u32[]{:S(2)}, u32[]{:S(2)}) collective-permute-start(bf16[1024,512]{1,0:T(8,128)(2,1)} %own.3), channel_id=1, source_target_pairs={{9,11},{11,13},{13,15},{2,0},{4,2},{6,4},{25,27},{27,29},{29,31},{... | collective-permute-start | bytes 3145736 | tf_op jit(solution)/shard_map/ppermute | solution.py:215
  5.0 1.3 %collective-permute-start.2 = (bf16[1024,512]{1,0:T(8,128)(2,1)}, bf16[1024,512]{1,0:T(8,128)(2,1)S(1)}, u32[]{:S(2)}, u32[]{:S(2)}) collective-permute-start(bf16[1024,512]{1,0:T(8,128)(2,1)} %own.3), channel_id=1, source_target_pairs={{10,9},{12,11},{14,13},{1,2},{3,4},{5,6},{26,25},{28,27},{30,29},{... | collective-permute-start | bytes 3145736 | tf_op jit(solution)/shard_map/ppermute | solution.py:217
  6.3 0.0 copy-start.1
  6.3 1.2 %copy-done.1 = bf16[1024,512]{1,0:T(8,128)(2,1)S(1)} copy-done((bf16[1024,512]{1,0:T(8,128)(2,1)S(1)}, bf16[1024,512]{1,0:T(8,128)(2,1)}, u32[]{:S(2)}) %copy-start.1) | copy-done | bytes 1048600
  7.5 0.0 copy-start.3
  7.5 0.7 copy-done.3
  8.2 0.0 copy-start.2
  8.2 1.7 %own_window.1 = (s32[16]{0:T(128)S(1)}, bf16[448,1024]{1,0:T(8,128)(2,1)S(1)}, bf16[64,1024]{1,0:T(8,128)(2,1)S(1)}) custom-call(s32[16,32]{1,0:T(8,128)S(1)} %bitcast.3, bf16[1024,512]{1,0:T(8,128)(2,1)S(1)} %copy-done.1), custom_call_target="tpu_custom_call" | custom-call | tf_op jit(solution)/shard_map/own_window/pallas_call | solution.py:218
  9.9 0.0 collective-permute-done.other
  9.9 1.2 %late_window.1 = bf16[448,1024]{1,0:T(8,128)(2,1)S(1)} custom-call(s32[16]{0:T(128)S(1)} %get-tuple-element.7.plan, bf16[448,1024]{1,0:T(8,128)(2,1)S(1)} %get-tuple-element.11.own, bf16[1024,512]{1,0:T(8,128)(2,1)S(1)} %collective-permute-done.other), custom_call_target="tpu_custom_call" | custom-call | tf_op jit(solution)/shard_map/late_window/pallas_call | solution.py:226
  11.1 2.5 %collective-permute-start.4 = (bf16[448,1024]{1,0:T(8,128)(2,1)S(1)}, bf16[448,1024]{1,0:T(8,128)(2,1)S(1)}, u32[]{:S(2)}, u32[]{:S(2)}) collective-permute-start(bf16[448,1024]{1,0:T(8,128)(2,1)S(1)} %late_window.1), channel_id=1, source_target_pairs={{6,8},{8,10},{10,12},{12,14},{3,1},{5,3},{7,5},{9,7},{22,24},{24,2... | collective-permute-start | bytes 2752520 | tf_op jit(solution)/shard_map/ppermute | solution.py:234
  13.6 1.3 %collective-permute-start.1 = (bf16[64,1024]{1,0:T(8,128)(2,1)S(1)}, bf16[64,1024]{1,0:T(8,128)(2,1)S(1)}, u32[]{:S(2)}, u32[]{:S(2)}) collective-permute-start(bf16[64,1024]{1,0:T(8,128)(2,1)S(1)} %get-tuple-element.9), channel_id=1, source_target_pairs={{7,9},{8,6},{23,25},{24,22},{39,41},{40,38},{55,57},{56,54},{71,73... | collective-permute-start | bytes 393224 | tf_op jit(solution)/shard_map/ppermute | solution.py:235
  14.9 0.0 copy-done.2
  14.9 0.0 copy-start
  14.9 7.1 %hidden_grad.1 = (bf16[1024,512]{1,0:T(8,128)(2,1)}, bf16[448,1024]{1,0:T(8,128)(2,1)S(1)}) custom-call(s32[16]{0:T(128)S(1)} %get-tuple-element.7.plan, bf16[1024,2048]{1,0:T(8,128)(2,1)} %grad.3, bf16[512,2048]{1,0:T(8,128)(2,1)} %bitcast.5, bf16[1024,512]{1,0:T(8,128)(2,1)S(1)} %copy-done.2, bf16[1024,512]{1,0:T(8,128)(2,1)S(1)} %collective-permute-done.other), custom_call_target="tpu_custom_call" | custom-call | flops 3087007744 | bytes 16777216 | tf_op jit(solution)/shard_map/hidden_grad/pallas_call | solution.py:238
  22.0 2.3 %collective-permute-done.1.middle = bf16[64,1024]{1,0:T(8,128)(2,1)S(1)} collective-permute-done((bf16[64,1024]{1,0:T(8,128)(2,1)S(1)}, bf16[64,1024]{1,0:T(8,128)(2,1)S(1)}, u32[]{:S(2)}, u32[]{:S(2)}) %collective-permute-start.1) | collective-permute-done | bytes 131104 | tf_op jit(solution)/shard_map/ppermute | solution.py:235
  24.3 0.0 collective-permute-done.3.early
  24.3 0.0 collective-permute-done.2.light
  24.3 1.3 %merge.1.local = bf16[448,1024]{1,0:T(8,128)(2,1)S(1)} custom-call(s32[16]{0:T(128)S(1)} %get-tuple-element.7.plan, bf16[64,1024]{1,0:T(8,128)(2,1)S(1)} %collective-permute-done.1.middle, bf16[1024,512]{1,0:T(8,128)(2,1)S(1)} %collective-permute-done.2.light, bf16[1024,512]{1,0:T(8,128)(2,1)S(1)} %collective-permute-done.3.early, ...), custom_call_target="tpu_custom_call" | custom-call | tf_op jit(solution)/shard_map/merge/pallas_call | solution.py:249
  25.6 0.3 collective-permute-done.4.late
  25.9 0.0 copy-done
  25.9 2.6 %partial.1 = s16[8,912,128]{2,1,0:T(8,128)(2,1)S(1)} custom-call(bf16[1024,2048]{1,0:T(8,128)(2,1)S(1)} %copy-done, bf16[448,1024]{1,0:T(8,128)(2,1)S(1)} %merge.1.local, bf16[448,1024]{1,0:T(8,128)(2,1)S(1)} %collective-permute-done.4.late), custom_call_target="tpu_custom_call" | custom-call | tf_op jit(solution)/shard_map/partial/pallas_call | solution.py:257
  28.5 31.6 %all_to_all.10.got = s16[8,912,128]{2,1,0:T(8,128)(2,1)S(1)} all-to-all(s16[8,912,128]{2,1,0:T(8,128)(2,1)S(1)} %partial.1), channel_id=1, replica_groups={{0,16,32,48,64,80,96,112},{128,144,160,176,192,208,224,240},{256,272,28..., dimensions={0} | all-to-all | bytes 3735552 | tf_op jit(solution)/shard_map/all_to_all | solution.py:266
  60.0 0.6 middle.1
  60.6 19.9 %all_to_all.11.got = s16[4,240,128]{2,1,0:T(8,128)(2,1)S(1)} all-to-all(s16[4,240,128]{2,1,0:T(8,128)(2,1)S(1)} %middle.1), channel_id=1, replica_groups={{0,128,256,384},{16,144,272,400},{32,160,288,416},{48,176,304,432},{64,..., dimensions={0} | all-to-all | bytes 491520 | tf_op jit(solution)/shard_map/all_to_all | solution.py:278
  80.5 0.8 %final.1 = f32[64,448]{1,0:T(8,128)} custom-call(s16[4,240,128]{2,1,0:T(8,128)(2,1)S(1)} %all_to_all.11.got), custom_call_target="tpu_custom_call" | custom-call | tf_op jit(solution)/shard_map/final/pallas_call | solution.py:281
Async XLA Ops:
  0.6 9.2 %collective-permute-start = (bf16[1024,512]{1,0:T(8,128)(2,1)}, bf16[1024,512]{1,0:T(8,128)(2,1)S(1)}, u32[]{:S(2)}, u32[]{:S(2)}) collective-permute-start(bf16[1024,512]{1,0:T(8,128)(2,1)} %own.3), channel_id=1, source_target_pairs={{0,1},{1,0},{2,3},{3,2},{4,5},{5,4},{6,7},{7,6},{8,9},{9,8},{10,11... | collective-permute-start | bytes 3145736 | tf_op jit(solution)/shard_map/ppermute | solution.py:216
  2.6 21.7 %collective-permute-start.3 = (bf16[1024,512]{1,0:T(8,128)(2,1)}, bf16[1024,512]{1,0:T(8,128)(2,1)S(1)}, u32[]{:S(2)}, u32[]{:S(2)}) collective-permute-start(bf16[1024,512]{1,0:T(8,128)(2,1)} %own.3), channel_id=1, source_target_pairs={{9,11},{11,13},{13,15},{2,0},{4,2},{6,4},{25,27},{27,29},{29,31},{... | collective-permute-start | bytes 3145736 | tf_op jit(solution)/shard_map/ppermute | solution.py:215
  5.0 19.3 %collective-permute-start.2 = (bf16[1024,512]{1,0:T(8,128)(2,1)}, bf16[1024,512]{1,0:T(8,128)(2,1)S(1)}, u32[]{:S(2)}, u32[]{:S(2)}) collective-permute-start(bf16[1024,512]{1,0:T(8,128)(2,1)} %own.3), channel_id=1, source_target_pairs={{10,9},{12,11},{14,13},{1,2},{3,4},{5,6},{26,25},{28,27},{30,29},{... | collective-permute-start | bytes 3145736 | tf_op jit(solution)/shard_map/ppermute | solution.py:217
  6.3 1.2 %copy-start.1 = (bf16[1024,512]{1,0:T(8,128)(2,1)S(1)}, bf16[1024,512]{1,0:T(8,128)(2,1)}, u32[]{:S(2)}) copy-start(bf16[1024,512]{1,0:T(8,128)(2,1)} %own.3) | copy-start | bytes 3145732
  7.5 0.7 copy-start.3
  8.2 6.7 %copy-start.2 = (bf16[1024,512]{1,0:T(8,128)(2,1)S(1)}, bf16[1024,512]{1,0:T(8,128)(2,1)}, u32[]{:S(2)}) copy-start(bf16[1024,512]{1,0:T(8,128)(2,1)} %own.3) | copy-start | bytes 3145732
  11.1 14.8 %collective-permute-start.4 = (bf16[448,1024]{1,0:T(8,128)(2,1)S(1)}, bf16[448,1024]{1,0:T(8,128)(2,1)S(1)}, u32[]{:S(2)}, u32[]{:S(2)}) collective-permute-start(bf16[448,1024]{1,0:T(8,128)(2,1)S(1)} %late_window.1), channel_id=1, source_target_pairs={{6,8},{8,10},{10,12},{12,14},{3,1},{5,3},{7,5},{9,7},{22,24},{24,2... | collective-permute-start | bytes 2752520 | tf_op jit(solution)/shard_map/ppermute | solution.py:234
  13.6 10.6 %collective-permute-start.1 = (bf16[64,1024]{1,0:T(8,128)(2,1)S(1)}, bf16[64,1024]{1,0:T(8,128)(2,1)S(1)}, u32[]{:S(2)}, u32[]{:S(2)}) collective-permute-start(bf16[64,1024]{1,0:T(8,128)(2,1)S(1)} %get-tuple-element.9), channel_id=1, source_target_pairs={{7,9},{8,6},{23,25},{24,22},{39,41},{40,38},{55,57},{56,54},{71,73... | collective-permute-start | bytes 393224 | tf_op jit(solution)/shard_map/ppermute | solution.py:235
  14.9 10.9 %copy-start = (bf16[1024,2048]{1,0:T(8,128)(2,1)S(1)}, bf16[1024,2048]{1,0:T(8,128)(2,1)}, u32[]{:S(2)}) copy-start(bf16[1024,2048]{1,0:T(8,128)(2,1)} %grad.3) | copy-start | bytes 12582916
